TPU v7x, 32 devices: a whole 2x2x4 slice. The times are simulated.
32 devices in a mesh: req: 4 (over z), row: 2 (over y), col: 4 (over x, core).
Axes of the slice: x: 2, y: 2, z: 4, core: 2. Of those that a mesh axis runs over, the one named last changes fastest.
Arguments:
- tokens: bfloat16 [8192, 2, 1792], P(('req', 'row'), None, 'col'), may hold values from -6 to 6
- w_query: bfloat16 [1792, 256], P('col', 'row'), may hold values from -0.125 to 0.125
- w_key: bfloat16 [1792, 256], P('col', 'row'), may hold values from -0.125 to 0.125
- w_value: bfloat16 [16, 200704], P('row', 'col'), may hold values from -0.125 to 0.125
- w_out: bfloat16 [1792, 1792], P('row', 'col'), may hold values from -0.125 to 0.125
- cached_state: bfloat16 [16, 273, 57344], P(('req', 'col'), None, 'row'), may hold values from -24 to 24
- cached_norm: bfloat16 [512, 273, 16], P(('req', 'col'), None, 'row'), as said below
- slot_prompt: int32 [512], P(('req', 'col')), may hold values from 0 to 511, as said below
- prompt_of: int32 [8192], P(('req', 'col')), may hold values from 0 to 511, as said below
- tail_keys: bfloat16 [8192, 2048], P(('req', 'col'), 'row'), may hold values from -6 to 6
- tail_values: bfloat16 [8192, 14336], P(('req', 'col'), 'row'), may hold values from -6 to 6
- tail_length: int32 [8192], P(('req', 'col')), may hold values from 0 to 8, as said below
Outputs:
- layer_out: bfloat16 [8192, 2, 1792], P(('req', 'row'), None, 'col')
Inputs may be any that keep to these rules, and one draw needn't show every extreme that they name: `slot_prompt`: each prompt sits in exactly one slot. The h-th block of 32 slots (holder h) keeps exactly 16 of its own prompts h * 32 to (h + 1) * 32 - 1; its other slots hold prompts of other holders, at most 2 of any one holder. The bound 2 is reached: some holder keeps 2 of one other holder's prompts. `prompt_of`: the h-th aligned block of 512 continuations holds exactly 16 continuations of each prompt h * 32 to (h + 1) * 32 - 1. `tail_length`: each aligned block of 512 continuations holds at least one continuation with a tail of 8 tokens. `cached_norm`: each prompt's column for a head is a sum of phi of some key vectors with positive weights.
All inputs are finite; a program needn't handle non-finite values.
Results may differ from a plain program's by a relative error of at most 0.019.
Values may be sent and summed in bfloat16 or wider, within the bound.
A program may use at most 192 MiB of HBM per device.

v0:
```python
import jax
import jax.numpy as jnp
from jax import lax
from jax.sharding import PartitionSpec as P

FEAT = 16
HEAD_DIM = 112


def features(values):
    feature_width = values.shape[-1]
    linear = values * feature_width ** (-0.25)
    square = (values[..., :, None] * values[..., None, :]).reshape(
        values.shape[:-1] + (feature_width * feature_width,)
    )
    square = square * (0.5**0.5 / feature_width**0.5)
    unit_column = jnp.ones(values.shape[:-1] + (1,), values.dtype)
    return jnp.concatenate([unit_column, linear, square], axis=-1)


def kernel_weight(scores):
    return 1.0 + scores + 0.5 * scores * scores


def prompt_terms(query_features, states, norms):
    numerator = jnp.einsum(
        "pcthf,pfhv->pcthv",
        query_features.astype(jnp.bfloat16),
        states,
        preferred_element_type=jnp.float32,
    )
    denominator = jnp.einsum(
        "pcthf,pfh->pcth",
        query_features,
        norms.astype(jnp.float32),
        precision=lax.Precision.HIGHEST,
    )
    return (numerator, denominator)


def body(
    tokens,
    w_query,
    w_key,
    w_value,
    w_out,
    cached_state,
    cached_norm,
    slot_prompt,
    prompt_of,
    tail_keys,
    tail_values,
    tail_length,
):
    heads_here = w_query.shape[1] // FEAT
    col_rows = w_query.shape[0]
    value_weight = jnp.moveaxis(w_value.reshape(heads_here, col_rows, HEAD_DIM), 0, 1).reshape(
        col_rows, heads_here * HEAD_DIM
    )
    stacked = jnp.concatenate([w_query, w_key, value_weight], axis=1)
    partial_value = jnp.einsum(
        "ctd,de->cte",
        lax.all_gather(tokens, "row", axis=0, tiled=True),
        stacked,
        preferred_element_type=jnp.float32,
    )
    projected = lax.psum_scatter(
        partial_value.astype(jnp.bfloat16), "col", scatter_dimension=0, tiled=True
    )
    cont_count = projected.shape[0]
    split_at = heads_here * FEAT
    queries = projected[:, :, :split_at].reshape(cont_count, 2, heads_here, FEAT)
    key_new = projected[:, :, split_at : 2 * split_at].reshape(cont_count, 2, heads_here, FEAT)
    value_new = projected[:, :, 2 * split_at :].reshape(cont_count, 2, heads_here, HEAD_DIM)
    local_width = heads_here * HEAD_DIM
    taylor = cached_state.shape[1]
    prompts_here = cached_state.shape[2] // local_width
    slot_rows = jnp.moveaxis(cached_state[0].reshape(taylor, local_width, prompts_here), 2, 0)
    per_prompt = cont_count // prompts_here
    holders = lax.axis_size(("req", "col"))
    capacity = (prompts_here // 2 + holders - 2) // (holders - 1)
    own_index = lax.axis_index(("req", "col"))
    own_prompts = own_index * prompts_here + jnp.arange(prompts_here, dtype=jnp.int32)
    ordering = jnp.argsort(prompt_of, stable=True)
    restore = jnp.argsort(ordering, stable=True)
    grouped = queries[ordering].reshape(prompts_here, per_prompt, 2, heads_here, FEAT)
    query_features = features(grouped.astype(jnp.float32))
    earlier = jnp.arange(prompts_here)[None, :] < jnp.arange(prompts_here)[:, None]
    outgoing = jnp.arange(holders * capacity)[:, None]
    owners = slot_prompt // prompts_here
    leaving = owners != own_index
    position = jnp.sum((owners[None, :] == owners[:, None]) & earlier & leaving[None, :], axis=1)
    chosen = (outgoing == (owners * capacity + position)[None, :]) & leaving[None, :]
    chosen_bf = chosen.astype(jnp.bfloat16)
    send_state = jnp.einsum(
        "sj,jfd->sfd", chosen_bf, slot_rows, preferred_element_type=jnp.float32
    ).astype(jnp.bfloat16)
    send_norm = jnp.einsum(
        "sj,jfh->sfh", chosen_bf, cached_norm, preferred_element_type=jnp.float32
    ).astype(jnp.bfloat16)
    send_ids = jnp.max(jnp.where(chosen, slot_prompt[None, :], -1), axis=1)
    got_state, got_norm, got_ids = (
        lax.all_to_all(
            send_state.reshape((holders, capacity) + send_state.shape[1:]),
            ("req", "col"),
            split_axis=0,
            concat_axis=0,
            tiled=True,
        ),
        lax.all_to_all(
            send_norm.reshape((holders, capacity) + send_norm.shape[1:]),
            ("req", "col"),
            split_axis=0,
            concat_axis=0,
            tiled=True,
        ),
        lax.all_to_all(
            send_ids.reshape(holders, capacity),
            ("req", "col"),
            split_axis=0,
            concat_axis=0,
            tiled=True,
        ),
    )
    pool_state = jnp.concatenate(
        [slot_rows, got_state.reshape((holders * capacity,) + slot_rows.shape[1:])], axis=0
    )
    pool_norm = jnp.concatenate(
        [cached_norm, got_norm.reshape((holders * capacity,) + cached_norm.shape[1:])], axis=0
    )
    pool_ids = jnp.concatenate([jnp.where(leaving, -1, slot_prompt), got_ids.reshape(-1)])
    located = jnp.argmax(pool_ids[None, :] == own_prompts[:, None], axis=1)
    prompt_num, prompt_den = prompt_terms(
        query_features,
        pool_state[located].reshape(prompts_here, taylor, heads_here, HEAD_DIM),
        pool_norm[located],
    )
    numerator = prompt_num.reshape(cont_count, 2, heads_here, HEAD_DIM)[restore]
    denominator = prompt_den.reshape(cont_count, 2, heads_here)[restore]
    scale = FEAT ** (-0.5)
    tail_count = tail_keys.shape[1] // (heads_here * FEAT)
    keys_tail = tail_keys.reshape(cont_count, heads_here, tail_count, FEAT)
    values_tail = tail_values.reshape(cont_count, heads_here, tail_count, HEAD_DIM)
    tail_scores = (
        jnp.einsum("cthf,chuf->cthu", queries, keys_tail, preferred_element_type=jnp.float32)
        * scale
    )
    live_mask = (jnp.arange(tail_count)[None, :] < tail_length[:, None]).astype(jnp.float32)
    tail_kernel = kernel_weight(tail_scores) * live_mask[:, None, None, :]
    new_scores = (
        jnp.einsum("cthf,cjhf->cthj", queries, key_new, preferred_element_type=jnp.float32) * scale
    )
    causal = (jnp.arange(2)[:, None] >= jnp.arange(2)[None, :]).astype(jnp.float32)
    new_kernel = kernel_weight(new_scores) * causal[None, :, None, :]
    numerator = numerator + jnp.einsum(
        "cthu,chuv->cthv",
        tail_kernel.astype(jnp.bfloat16),
        values_tail,
        preferred_element_type=jnp.float32,
    )
    numerator = numerator + jnp.einsum(
        "cthj,cjhv->cthv",
        new_kernel.astype(jnp.bfloat16),
        value_new,
        preferred_element_type=jnp.float32,
    )
    denominator = denominator + jnp.sum(tail_kernel, axis=-1) + jnp.sum(new_kernel, axis=-1)
    heads_out = (
        (numerator / denominator[..., None])
        .astype(jnp.bfloat16)
        .reshape(cont_count, 2, heads_here * HEAD_DIM)
    )
    terms = jnp.einsum(
        "cte,ed->ctd",
        lax.all_gather(heads_out, "col", axis=0, tiled=True),
        w_out,
        preferred_element_type=jnp.float32,
    )
    mixed = lax.psum_scatter(
        terms.astype(jnp.bfloat16), "row", scatter_dimension=0, tiled=True
    ).astype(jnp.float32)
    return (mixed + tokens.astype(jnp.float32)).astype(jnp.bfloat16)


def solution(mesh):
    return jax.shard_map(
        body,
        mesh=mesh,
        in_specs=(
            P(("req", "row"), None, "col"),
            P("col", "row"),
            P("col", "row"),
            P("row", "col"),
            P("row", "col"),
            P(("req", "col"), None, "row"),
            P(("req", "col"), None, "row"),
            P(("req", "col")),
            P(("req", "col")),
            P(("req", "col"), "row"),
            P(("req", "col"), "row"),
            P(("req", "col")),
        ),
        out_specs=P(("req", "row"), None, "col"),
        check_vma=False,
    )
```

profile of v0, /device:TPU:9, one launch (start us, length us, event | category | flops | bytes accessed | tf_op | source)
XLA Modules:
  0.0 732.4 jit_solution(14606894965510931050)
XLA Ops:
  18.2 23.8 %copy.156 = bf16[1,273,28672]{1,2,0:T(8,128)(2,1)} copy(bf16[1,273,28672]{2,1,0:T(8,128)(2,1)} %param.17) | data formatting | bytes 31309824 | tf_op args[5]
  42.0 29.2 %copy.158 = bf16[32,273,896]{2,0,1:T(8,128)(2,1)} copy(bf16[32,273,896]{1,0,2:T(8,128)(2,1)} %bitcast.79) | data formatting | bytes 31309824 | tf_op jit(solution)/shard_map/transpose | solution.py:78
  77.4 11.0 %convolution_convert_fusion.1 = bf16[32,273,896]{2,0,1:T(8,128)(2,1)} fusion(bf16[32,273,896]{2,0,1:T(8,128)(2,1)} %copy.158, s32[32]{0:T(128)S(1)} %multiply_add_fusion, pred[32]{0:T(512)(128)(4,1)S(1)} %get-tuple-element.12), kind=kOutput, calls=%fused_computation.11 | convolution fusion | flops 508786688 | bytes 31309984 | tf_op jit(solution)/shard_map/sj,jfd->sfd/dot_general | solution.py:95
  88.3 30.9 %reshape.121 = bf16[16,2,273,896]{3,1,0,2:T(2,128)(2,1)} reshape(bf16[32,273,896]{2,0,1:T(8,128)(2,1)} %convolution_convert_fusion.1) | data formatting | bytes 31309824 | tf_op jit(solution)/shard_map/reshape | solution.py:104
  119.3 13.9 %copy.159 = bf16[16,2,273,896]{3,1,2,0:T(2,128)(2,1)} copy(bf16[16,2,273,896]{3,1,0,2:T(2,128)(2,1)} %reshape.121) | data formatting | bytes 31309824 | tf_op jit(solution)/shard_map/reshape | solution.py:104
  142.2 9.4 %fusion.4 = bf16[2048,2,1152]{0,2,1:T(8,128)(2,1)} fusion(bf16[2048,2,448]{0,2,1:T(8,128)(2,1)} %all-gather.3.cloned.1.call-done, bf16[448,896]{1,0:T(8,128)(2,1)S(1)} %reshape.126, bf16[448,128]{1,0:T(8,128)(2,1)S(1)} %copy-done.8, bf16[448,128]{1,0:T(8,128)(2,1)S(1)} %copy-done.9), kind=kOutput, calls=%fused_computation.14 | convolution fusion | flops 4235673600 | bytes 14139392 | tf_op jit(solution)/shard_map/ctd,de->cte/dot_general | solution.py:61
  153.3 12.0 %copy.175 = bf16[512,8,8,16]{3,2,1,0:T(8,128)(2,1)} copy(bf16[512,8,8,16]{0,3,2,1:T(8,128)(2,1)S(1)} %bitcast.90) | data formatting | bytes 2097152 | tf_op jit(solution)/shard_map/reshape | solution.py:142
  165.3 10.8 %copy.178 = bf16[512,7168]{0,1:T(8,128)(2,1)} copy(bf16[512,7168]{1,0:T(8,128)(2,1)} %param.22) | data formatting | bytes 14680064 | tf_op args[10]
  176.1 11.8 %copy.180 = bf16[512,8,8,112]{3,2,1,0:T(8,128)(2,1)} copy(bf16[512,8,8,112]{0,3,2,1:T(8,128)(2,1)} %bitcast.84) | data formatting | bytes 14680064 | tf_op jit(solution)/shard_map/reshape | solution.py:143
  187.9 26.9 %copy.157 = bf16[273,896,32]{1,0,2:T(8,128)(2,1)} copy(bf16[273,896,32]{0,2,1:T(8,128)(2,1)} %bitcast.80) | data formatting | bytes 31309824 | tf_op jit(solution)/shard_map/reshape;squeeze | solution.py:78
  225.2 55.6 %reduce-scatter.3.cloned.1.call-done = bf16[512,2,1152]{0,2,1:T(8,128)(2,1)} async-done(((bf16[2048,2,1152]{0,2,1:T(8,128)(2,1)}), bf16[512,2,1152]{0,2,1:T(8,128)(2,1)}) %reduce-scatter.3.cloned.1.call-update) | async-done | bytes 2359312 | tf_op jit(solution)/shard_map/reduce_scatter | solution.py:67
  367.6 8.9 %fusion.41 = f32[512,8,2,112]{3,2,1,0:T(2,128)} fusion(bf16[512,2,8,8]{3,1,2,0:T(2,128)(2,1)} %copy.179, bf16[512,8,8,112]{3,2,1,0:T(8,128)(2,1)} %copy.180), kind=kOutput, calls=%fused_computation.81 | convolution fusion | flops 14680064 | bytes 11141120 | tf_op jit(solution)/shard_map/cthu,chuv->cthv/dot_general | solution.py:155
  383.6 11.6 %multiply_multiply_fusion = f32[32,16,2,8,16,16]{0,5,4,3,2,1:T(8,128)} fusion(f32[32,16,2,8,16]{0,4,3,2,1:T(8,128)S(1)} %copy.166), kind=kLoop, calls=%fused_computation.5 | loop fusion | flops 4194304 | bytes 8912896 | tf_op jit(solution)/shard_map/mul | solution.py:16
  395.1 22.5 %copy.170 = f32[32,16,2,8,256]{4,1,2,3,0:T(8,128)} copy(f32[32,16,2,8,256]{0,4,3,2,1:T(8,128)} %bitcast.81) | data formatting | bytes 16777216 | tf_op jit(solution)/shard_map/mul | solution.py:16
  417.7 32.5 %fusion.2 = f32[32,8,1,16,2]{3,2,4,1,0:T(1,128)S(1)} fusion(f32[32,16,2,8,256]{4,1,2,3,0:T(8,128)} %copy.170, f32[32,16,2,8,16]{4,1,2,3,0:T(8,128)} %copy.169, f32[273]{0:T(512)S(1)} %pad.2.clone, bf16[32,273,8,1,1]{1,2,0,3,4:T(8,128)(2,1)S(1)} %bitcast.85), kind=kOutput, calls=%fused_computation.12 | convolution fusion | flops 31309824 | bytes 9086532 | tf_op jit(solution)/shard_map/pcthf,pfh->pcth/dot_general | solution.py:32
  453.2 22.2 %all-to-all-done = bf16[16,2,273,896]{3,1,2,0:T(2,128)(2,1)} async-done(((bf16[16,2,273,896]{3,1,2,0:T(2,128)(2,1)}), bf16[16,2,273,896]{3,1,2,0:T(2,128)(2,1)}, u32[]{:S(2)}, u32[]{:S(2)}) %all-to-all-start) | async-done | bytes 15654944 | tf_op jit(solution)/shard_map/all_to_all | solution.py:103
  475.4 15.2 %copy.160 = bf16[16,2,273,896]{3,2,1,0:T(8,128)(2,1)} copy(bf16[16,2,273,896]{3,1,2,0:T(2,128)(2,1)} %all-to-all-done) | data formatting | bytes 31309824 | tf_op jit(solution)/shard_map/all_to_all | solution.py:103
  490.6 21.9 %pad_maximum_fusion = bf16[64,273,896]{2,1,0:T(8,128)(2,1)} fusion(bf16[32,273,896]{2,1,0:T(8,128)(2,1)} %bitcast.83, bf16[32,273,896]{2,1,0:T(8,128)(2,1)} %bitcast.82), kind=kLoop, calls=%fused_computation.6 | loop fusion | flops 15654912 | bytes 62619648 | tf_op jit(solution)/shard_map/concatenate | solution.py:125
  512.5 11.6 %gather_fusion = bf16[32,273,896]{2,1,0:T(8,128)(2,1)} fusion(bf16[64,273,896]{2,1,0:T(8,128)(2,1)} %pad_maximum_fusion, s32[1024]{0:T(1024)S(1)} %pad_clamp_fusion.2), kind=kCustom, calls=%fused_computation | custom fusion | bytes 31309952 | tf_op jit(solution)/shard_map/gather | solution.py:135
  524.1 32.1 %reshape.189 = bf16[32,273,8,112]{3,2,1,0:T(8,128)(2,1)} reshape(bf16[32,273,896]{2,1,0:T(8,128)(2,1)} %gather_fusion) | data formatting | bytes 31309824 | tf_op jit(solution)/shard_map/reshape | solution.py:135
  556.2 13.7 %fusion.10 = f32[32,16,2,8,112]{4,1,2,3,0:T(8,128)S(1)} fusion(f32[32,16,2,8,256]{4,1,2,3,0:T(8,128)} %copy.170, f32[32,16,2,8,16]{4,1,2,3,0:T(8,128)} %copy.169, f32[273]{0:T(512)S(1)} %pad.2.clone, bf16[32,273,8,112,1]{3,2,1,0,4:T(8,128)(2,1)} %bitcast.86), kind=kOutput, calls=%fused_computation.23 | convolution fusion | flops 514375680 | bytes 28238916 | tf_op jit(solution)/shard_map/pcthf,pfhv->pcthv/dot_general | solution.py:26
  594.3 69.4 %all-gather.5.cloned.1.call-done = bf16[2048,2,896]{2,0,1:T(8,128)(2,1)} async-done(((bf16[512,2,896]{2,0,1:T(8,128)(2,1)}), bf16[2048,2,896]{2,0,1:T(8,128)(2,1)}) %all-gather.5.cloned.1.call-update) | async-done | bytes 7340048 | tf_op jit(solution)/shard_map/all_gather | solution.py:175
  663.7 9.4 %convolution_convert_fusion.2 = bf16[2048,2,448]{0,2,1:T(8,128)(2,1)} fusion(bf16[2048,2,896]{2,0,1:T(8,128)(2,1)} %all-gather.5.cloned.1.call-done, bf16[896,448]{0,1:T(8,128)(2,1)S(1)} %copy-done), kind=kOutput, calls=%fused_computation.22 | convolution fusion | flops 3290169344 | bytes 11812864 | tf_op jit(solution)/shard_map/cte,ed->ctd/dot_general | solution.py:173
  673.1 48.8 %reduce-scatter.5.cloned.1.call-done = bf16[1024,2,448]{0,2,1:T(8,128)(2,1)} async-done(((bf16[2048,2,448]{0,2,1:T(8,128)(2,1)}), bf16[1024,2,448]{0,2,1:T(8,128)(2,1)}) %reduce-scatter.5.cloned.1.call-update) | async-done | bytes 1835024 | tf_op jit(solution)/shard_map/reduce_scatter | solution.py:179
  (103 shorter events, 163.5 us)
Async XLA Ops:
  6.5 657.2 %copy-start = (bf16[896,448]{0,1:T(8,128)(2,1)S(1)}, bf16[896,448]{0,1:T(8,128)(2,1)}, u32[]{:S(2)}) copy-start(bf16[896,448]{0,1:T(8,128)(2,1)} %param.16) | copy-start | bytes 2408452
  6.5 135.6 %all-gather.3.cloned.1.call-start = ((), (), s32[]{:S(2)}) async-start(), calls=%async_computation.5 | async-start | bytes 5505024 | tf_op jit(solution)/shard_map/all_gather | solution.py:63
  9.6 61.7 %all-to-all-start.1 = ((s32[16,1,2]{2,1,0:T(1,128)}), s32[16,1,2]{2,1,0:T(1,128)S(1)}, u32[]{:S(2)}, u32[]{:S(2)}) async-start(s32[16,1,2]{2,1,0:T(1,128)} %bitcast.5), calls=%async_computation.1 | async-start | bytes 16384 | tf_op jit(solution)/shard_map/all_to_all | solution.py:117
  71.3 61.9 %all-to-all-start.2 = ((bf16[16,2,273,8]{2,1,3,0:T(2,128)(2,1)}), bf16[16,2,273,8]{2,1,3,0:T(2,128)(2,1)S(1)}, u32[]{:S(2)}, u32[]{:S(2)}) async-start(bf16[16,2,273,8]{2,1,3,0:T(2,128)(2,1)} %copy.191), calls=%async_computation.3 | async-start | bytes 393216 | tf_op jit(solution)/shard_map/all_to_all | solution.py:110
  133.2 6.2 copy-start.4
  133.2 342.2 %all-to-all-start = ((bf16[16,2,273,896]{3,1,2,0:T(2,128)(2,1)}), bf16[16,2,273,896]{3,1,2,0:T(2,128)(2,1)}, u32[]{:S(2)}, u32[]{:S(2)}) async-start(bf16[16,2,273,896]{3,1,2,0:T(2,128)(2,1)} %copy.159), calls=%async_computation | async-start | bytes 31309824 | tf_op jit(solution)/shard_map/all_to_all | solution.py:103
  139.4 2.8 copy-start.8
  139.4 2.8 copy-start.9
  139.4 141.4 %reduce-scatter.3.cloned.1.call-start = ((), (), s32[]{:S(2)}) async-start(), calls=%async_computation.6 | async-start | bytes 11796480 | tf_op jit(solution)/shard_map/reduce_scatter | solution.py:67
  151.6 1.2 copy-start.2
  151.6 512.1 %all-gather.5.cloned.1.call-start = ((), (), s32[]{:S(2)}) async-start(), calls=%async_computation.7 | async-start | bytes 9175040 | tf_op jit(solution)/shard_map/all_gather | solution.py:175
  187.9 26.9 %copy-start.7 = (s32[512]{0:T(512)S(1)}, s32[512]{0:T(512)}, u32[]{:S(2)}) copy-start(s32[512]{0:T(512)} %param.20) | copy-start | bytes 6148
  187.9 34.5 %copy-start.6 = (s32[512]{0:T(512)S(1)}, s32[512]{0:T(512)}, u32[]{:S(2)}) copy-start(s32[512]{0:T(512)} %param.23) | copy-start | bytes 6148
  187.9 36.6 %copy-start.5 = (bf16[32,273,8]{1,2,0:T(8,128)(2,1)S(1)}, bf16[32,273,8]{1,2,0:T(8,128)(2,1)}, u32[]{:S(2)}) copy-start(bf16[32,273,8]{1,2,0:T(8,128)(2,1)} %param.18) | copy-start | bytes 419332
  288.4 9.2 %copy-start.3 = (bf16[512,2,128]{0,2,1:T(8,128)(2,1)S(1)}, bf16[512,2,128]{0,2,1:T(8,128)(2,1)}, u32[]{:S(2)}) copy-start(bf16[512,2,128]{0,2,1:T(8,128)(2,1)} %get-tuple-element.15) | copy-start | bytes 786436
  594.2 127.7 %reduce-scatter.5.cloned.1.call-start = ((), (), s32[]{:S(2)}) async-start(), calls=%async_computation.8 | async-start | bytes 5505024 | tf_op jit(solution)/shard_map/reduce_scatter | solution.py:179
  673.1 48.9 %copy-start.1 = (bf16[1024,2,448]{0,2,1:T(8,128)(2,1)S(1)}, bf16[1024,2,448]{0,2,1:T(8,128)(2,1)}, u32[]{:S(2)}) copy-start(bf16[1024,2,448]{0,2,1:T(8,128)(2,1)} %param.12) | copy-start | bytes 5505028
Sparse Core Ops, SparseCore 0:
  8.9 51.9 all-gather.2
  151.7 129.0 reduce-scatter.2
  594.3 69.2 all-gather.4
  673.2 48.6 reduce-scatter.4
where the time goes:
time: 747 us; the launch traced here: 732 us
  local copies, waits for them, and re-layouts  336 us (45%)
  waiting for transfers between devices  197 us (26%)
  matrix products  111 us (15%)
  other arithmetic  55.3 us (7%)
  starting transfers between devices  19.2 us (3%)
  between operations  13.9 us (2%)
    all_gather x1, waiting for transfers between devices, body(): lax.all_gather(heads_out, 'col', axis=0, tiled=True)  69.4 us
    reduce_scatter x1, waiting for transfers between devices, body(): lax.psum_scatter(partial_value.astype(jnp.bfloat16), 'col', scatter_dimen...  55.6 us
    reduce_scatter x1, waiting for transfers between devices, body(): lax.psum_scatter(terms.astype(jnp.bfloat16), 'row', scatter_dimension=0,...  48.8 us
    reshape x2, local copies, waits for them, and re-layouts, body(): send_state.reshape((holders, capacity) + send_state.shape[1:])  44.9 us
    unnamed x23, local copies, waits for them, and re-layouts  36.2 us
    dot_general x1, matrix products, prompt_terms(): jnp.einsum('pcthf,pfh->pcth', query_features, norms.astype(jnp.float32),...  32.5 us
    reshape x1, local copies, waits for them, and re-layouts, body(): pool_state[located].reshape(prompts_here, taylor, heads_here, HEAD_DIM)  32.1 us
    transpose x1, local copies, waits for them, and re-layouts, body(): jnp.moveaxis(cached_state[0].reshape(taylor, local_width, prompts_here),...  29.2 us
  transfers between devices with their start and end apart: 7, of which 4 were waited for; matrix products, arithmetic and copies ran while one was open for 50% of the time, Pallas kernels for 0%

commit v1 on v0

v1 whole, which is shorter than its diff:
```python
import functools

import jax
import jax.numpy as jnp
import numpy as np
from jax import lax
from jax.experimental import pallas as pl
from jax.experimental.pallas import tpu as pltpu
from jax.sharding import PartitionSpec as P

FEAT = 16
HEAD_DIM = 112
LANES = 128
TAYLOR_PAD = 384
F32 = jnp.float32
BF16 = jnp.bfloat16
VMEM_LIMIT = 48 * 1024 * 1024
CONTRACT_LAST = (((1,), (1,)), ((), ()))


def dot(a, b):
    return jnp.dot(a, b, preferred_element_type=F32)


def kappa(s):
    return 1.0 + s + 0.5 * s * s


def split3(x):
    hi = x.astype(BF16)
    rest = x - hi.astype(F32)
    mid = rest.astype(BF16)
    return hi, mid, (rest - mid.astype(F32)).astype(BF16)


def state_kernel(perm_ref, state_ref, norm_ref, out_ref):
    slots = out_ref.shape[1]
    taylor = state_ref.shape[1]
    width = 8 * slots
    perm = perm_ref[...]
    out_ref[0, :, :, taylor:] = jnp.zeros((slots, LANES, TAYLOR_PAD - taylor), BF16)
    for pair in range(HEAD_DIM // 16):
        parts = []
        for half in range(2):
            lower = (2 * pair + half) * width
            turned = lax.dot_general(
                perm, state_ref[0, :, lower : lower + width], CONTRACT_LAST, preferred_element_type=F32
            )
            parts.append(turned.reshape(slots, 8, taylor))
        both = jnp.concatenate(parts, axis=1).astype(BF16)
        out_ref[0, :, pair * 16 : pair * 16 + 16, :taylor] = both
    norm = norm_ref[0].astype(F32)
    wide = jnp.broadcast_to(norm[:, None, :], (slots, 16, taylor)).astype(BF16)
    out_ref[0, :, HEAD_DIM:, :taylor] = wide


def turn_states(cached_state, norm, heads, slots):
    taylor = cached_state.shape[1]
    width = 8 * slots
    perm = np.zeros((width, width), np.float32)
    for v in range(8):
        for q in range(slots):
            perm[q * 8 + v, v * slots + q] = 1
    return pl.pallas_call(
        state_kernel,
        grid=(heads,),
        in_specs=[
            pl.BlockSpec((width, width), lambda h: (0, 0)),
            pl.BlockSpec((1, taylor, HEAD_DIM * slots), lambda h: (0, 0, h)),
            pl.BlockSpec((1, slots, taylor), lambda h: (h, 0, 0)),
        ],
        out_specs=pl.BlockSpec((1, slots, LANES, TAYLOR_PAD), lambda h: (h, 0, 0, 0)),
        out_shape=jax.ShapeDtypeStruct((heads, slots, LANES, TAYLOR_PAD), BF16),
        compiler_params=pltpu.CompilerParams(vmem_limit_bytes=VMEM_LIMIT),
        cost_estimate=pl.CostEstimate(
            flops=20_000_000_000, bytes_accessed=45_000_000, transcendentals=0
        ),
    )(jnp.asarray(perm, BF16), cached_state, norm)


def prompt_kernel(q_ref, pick_ref, shift_ref, states_ref, out_ref, phi_ref):
    rows = q_ref.shape[0]
    slots = states_ref.shape[1]
    per = rows // slots
    width = q_ref.shape[1] // 2
    pick = pick_ref[0]
    for t in range(2):
        both = dot(q_ref[:, t * width : (t + 1) * width], pick)
        left = both[:, :TAYLOR_PAD] + shift_ref[0:1]
        right = both[:, TAYLOR_PAD:] + shift_ref[1:2]
        phi = left * right * shift_ref[2:3]
        hi = phi.astype(BF16)
        phi_ref[t] = hi
        phi_ref[2 + t] = (phi - hi.astype(F32)).astype(BF16)
    lane = lax.broadcasted_iota(jnp.int32, (2 * per, LANES), 1)
    for q in range(slots):
        pieces = [phi_ref[k, q * per : (q + 1) * per, :] for k in range(4)]
        got = lax.dot_general(
            jnp.concatenate(pieces, axis=0), states_ref[0, q], CONTRACT_LAST, preferred_element_type=F32
        )
        top = got[: 2 * per]
        den = top + got[2 * per :]
        hi, mid, low = split3(den)
        res = jnp.where(lane < HEAD_DIM, top, hi.astype(F32))
        res = jnp.where(lane == HEAD_DIM + 1, mid.astype(F32), res)
        res = jnp.where(lane == HEAD_DIM + 2, low.astype(F32), res).astype(BF16)
        out_ref[q * per : (q + 1) * per, :LANES] = res[:per]
        out_ref[q * per : (q + 1) * per, LANES:] = res[per:]


def pick_tables(heads):
    pick = np.zeros((heads, heads * FEAT, 2 * TAYLOR_PAD), np.float32)
    shift = np.zeros((8, TAYLOR_PAD), np.float32)
    shift[0, 0] = 1
    shift[1, : FEAT + 1] = 1
    shift[2, 0] = 1
    shift[2, 1 : FEAT + 1] = FEAT ** (-0.25)
    shift[2, FEAT + 1 : FEAT + 1 + FEAT * FEAT] = 0.5**0.5 / FEAT**0.5
    for h in range(heads):
        for a in range(FEAT):
            pick[h, h * FEAT + a, 1 + a] = 1
            for b in range(FEAT):
                f = 1 + FEAT + a * FEAT + b
                pick[h, h * FEAT + a, f] = 1
                pick[h, h * FEAT + b, TAYLOR_PAD + f] = 1
    return jnp.asarray(pick, BF16), jnp.asarray(shift, F32)


def prompt_terms(slot_queries, states, heads, slots):
    rows = slot_queries.shape[0]
    pick, shift = pick_tables(heads)
    return pl.pallas_call(
        prompt_kernel,
        grid=(heads,),
        in_specs=[
            pl.BlockSpec(slot_queries.shape, lambda h: (0, 0)),
            pl.BlockSpec((1,) + pick.shape[1:], lambda h: (h, 0, 0)),
            pl.BlockSpec(shift.shape, lambda h: (0, 0)),
            pl.BlockSpec((1, slots, LANES, TAYLOR_PAD), lambda h: (h, 0, 0, 0)),
        ],
        out_specs=pl.BlockSpec((rows, 2 * LANES), lambda h: (0, h)),
        out_shape=jax.ShapeDtypeStruct((rows, heads * 2 * LANES), BF16),
        scratch_shapes=[pltpu.VMEM((4, rows, TAYLOR_PAD), BF16)],
        compiler_params=pltpu.CompilerParams(vmem_limit_bytes=VMEM_LIMIT),
    )(slot_queries, pick, shift, states)


def tail_kernel(heads, tail, q_ref, tk_ref, tv_ref, len_ref, eq, rq, ew, rv, dw, rn, en, pad, out_ref):
    hf = heads * FEAT
    hd = heads * HEAD_DIM
    total = 2 * hf + hd
    block = q_ref.shape[0]
    lane = lax.broadcasted_iota(jnp.int32, (block, heads * tail), 1)
    live = lax.rem(lane, tail) < len_ref[...]
    keys = tk_ref[...].astype(F32)
    scale = FEAT ** (-0.5)
    new_k = [q_ref[:, t * total + hf : t * total + 2 * hf].astype(F32) for t in range(2)]
    new_v = [dot(q_ref[:, t * total + 2 * hf : (t + 1) * total], pad[...]) for t in range(2)]
    for t in range(2):
        query = q_ref[:, t * total : t * total + hf]
        spread = dot(query, eq[...])
        scores = dot((spread * keys).astype(BF16), rq[...]) * scale
        weight = jnp.where(live, kappa(scores), 0.0)
        hi = weight.astype(BF16)
        low = (weight - hi.astype(F32)).astype(BF16)
        acc = dot(hi, dw[...]) + dot(low, dw[...])
        for i in range(t + 1):
            product = (query.astype(F32) * new_k[i]).astype(BF16)
            fresh = kappa(dot(product, rn[...]) * scale)
            fresh_hi = fresh.astype(BF16)
            fresh_low = (fresh - fresh_hi.astype(F32)).astype(BF16)
            spread_hi = dot(fresh_hi, en[0])
            acc = acc + spread_hi * new_v[i] + dot(fresh_hi, en[1]) + dot(fresh_low, en[1])
        span = tail * HEAD_DIM
        for h in range(heads):
            wide = dot(hi, ew[:, h * span : (h + 1) * span])
            product = wide * tv_ref[:, h * span : (h + 1) * span].astype(F32)
            summed = dot(product.astype(BF16), rv[...])
            at = (2 * h + t) * LANES
            out_ref[:, at : at + LANES] = acc[:, h * LANES : (h + 1) * LANES] + summed


def tail_tables(heads, tail):
    hf, hd = heads * FEAT, heads * HEAD_DIM
    eq = np.zeros((hf, heads * tail * FEAT), np.float32)
    rq = np.zeros((heads * tail * FEAT, heads * tail), np.float32)
    ew = np.zeros((heads * tail, heads * tail * HEAD_DIM), np.float32)
    rv = np.zeros((tail * HEAD_DIM, LANES), np.float32)
    dw = np.zeros((heads * tail, heads * LANES), np.float32)
    rn = np.zeros((hf, LANES), np.float32)
    en = np.zeros((2, LANES, heads * LANES), np.float32)
    pad = np.zeros((hd, heads * LANES), np.float32)
    entries = np.arange(HEAD_DIM)
    for u in range(tail):
        rv[u * HEAD_DIM + entries, entries] = 1
    for h in range(heads):
        en[0, h, h * LANES + entries] = 1
        en[1, h, h * LANES + HEAD_DIM] = 1
        pad[h * HEAD_DIM + entries, h * LANES + entries] = 1
        rn[h * FEAT : (h + 1) * FEAT, h] = 1
        for u in range(tail):
            k = h * tail + u
            ew[k, k * HEAD_DIM + entries] = 1
            dw[k, h * LANES + HEAD_DIM] = 1
            for a in range(FEAT):
                eq[h * FEAT + a, k * FEAT + a] = 1
                rq[k * FEAT + a, k] = 1
    return [jnp.asarray(x, BF16) for x in (eq, rq, ew, rv, dw, rn, en, pad)]


def tail_terms(projected, tail_keys, tail_values, tail_length, heads, tail):
    conts = projected.shape[0]
    block = min(conts, 128)
    tables = tail_tables(heads, tail)

    def rows(array):
        return pl.BlockSpec((block, array.shape[1]), lambda i: (i, 0))

    def whole(array):
        return pl.BlockSpec(array.shape, lambda i, n=array.ndim: (0,) * n)

    return pl.pallas_call(
        functools.partial(tail_kernel, heads, tail),
        grid=(conts // block,),
        in_specs=[rows(projected), rows(tail_keys), rows(tail_values), rows(tail_length)]
        + [whole(x) for x in tables],
        out_specs=pl.BlockSpec((block, heads * 2 * LANES), lambda i: (i, 0)),
        out_shape=jax.ShapeDtypeStruct((conts, heads * 2 * LANES), F32),
        compiler_params=pltpu.CompilerParams(vmem_limit_bytes=VMEM_LIMIT),
        cost_estimate=pl.CostEstimate(
            flops=20_000_000_000, bytes_accessed=25_000_000, transcendentals=0
        ),
    )(projected, tail_keys, tail_values, tail_length, *tables)


def combine_kernel(heads, acc_ref, sent_at, kept_at, got_ref, kept_ref, pack, out_ref):
    block = acc_ref.shape[0]
    hd = heads * HEAD_DIM
    sent = sent_at[...] == lax.broadcasted_iota(jnp.int32, (block, got_ref.shape[0]), 1)
    kept = kept_at[...] == lax.broadcasted_iota(jnp.int32, (block, kept_ref.shape[0]), 1)
    sent = sent.astype(F32).astype(BF16)
    kept = kept.astype(F32).astype(BF16)
    prompt = dot(sent, got_ref[...]) + dot(kept, kept_ref[...])
    for t in range(2):
        parts = []
        for h in range(heads):
            at = (2 * h + t) * LANES
            terms = prompt[:, at : at + LANES]
            total = acc_ref[:, at : at + LANES] + terms
            den = total[:, HEAD_DIM : HEAD_DIM + 1]
            den = den + terms[:, HEAD_DIM + 1 : HEAD_DIM + 2] + terms[:, HEAD_DIM + 2 : HEAD_DIM + 3]
            parts.append((total / den).astype(BF16))
        wide = jnp.concatenate(parts, axis=1)
        out_ref[:, t * hd : (t + 1) * hd] = dot(wide, pack[...]).astype(BF16)


def combine(acc, sent_at, kept_at, got, kept, heads):
    conts = acc.shape[0]
    block = min(conts, 128)
    hd = heads * HEAD_DIM
    pack = np.zeros((heads * LANES, hd), np.float32)
    entries = np.arange(HEAD_DIM)
    for h in range(heads):
        pack[h * LANES + entries, h * HEAD_DIM + entries] = 1

    def rows(array):
        return pl.BlockSpec((block, array.shape[1]), lambda i: (i, 0))

    def whole(array):
        return pl.BlockSpec(array.shape, lambda i: (0, 0))

    pack = jnp.asarray(pack, BF16)
    return pl.pallas_call(
        functools.partial(combine_kernel, heads),
        grid=(conts // block,),
        in_specs=[rows(acc), rows(sent_at), rows(kept_at), whole(got), whole(kept), whole(pack)],
        out_specs=pl.BlockSpec((block, 2 * hd), lambda i: (i, 0)),
        out_shape=jax.ShapeDtypeStruct((conts, 2 * hd), BF16),
        compiler_params=pltpu.CompilerParams(vmem_limit_bytes=VMEM_LIMIT),
    )(acc, sent_at, kept_at, got, kept, pack)


def body(
    tokens,
    w_query,
    w_key,
    w_value,
    w_out,
    cached_state,
    cached_norm,
    slot_prompt,
    prompt_of,
    tail_keys,
    tail_values,
    tail_length,
):
    heads = w_query.shape[1] // FEAT
    depth = w_query.shape[0]
    hf, hd = heads * FEAT, heads * HEAD_DIM
    slots = slot_prompt.shape[0]
    conts = prompt_of.shape[0]
    per = conts // slots
    tail = tail_keys.shape[1] // hf
    axes = ("req", "col")
    holders = lax.axis_size(axes)
    capacity = (slots // 2 + holders - 2) // (holders - 1)
    me = lax.axis_index(axes)

    every = lax.all_gather(slot_prompt, axes, axis=0, tiled=True)
    flat = tokens.reshape(tokens.shape[0], 2 * depth)
    gathered = lax.all_gather(flat, "row", axis=0, tiled=True)
    value_weight = jnp.moveaxis(w_value.reshape(heads, depth, HEAD_DIM), 0, 1).reshape(depth, hd)
    stacked = jnp.concatenate([w_query, w_key, value_weight], axis=1)
    partial_sums = jnp.concatenate(
        [dot(gathered[:, t * depth : (t + 1) * depth], stacked).astype(BF16) for t in range(2)], axis=1
    )
    projected = lax.psum_scatter(partial_sums, "col", scatter_dimension=0, tiled=True)
    states = turn_states(cached_state, jnp.transpose(cached_norm, (2, 0, 1)), heads, slots)

    owner = (every // slots).reshape(holders, slots)
    before = jnp.arange(slots)[None, :] < jnp.arange(slots)[:, None]
    position = jnp.sum((owner[:, :, None] == owner[:, None, :]) & before[None], axis=2).reshape(-1)
    block_of = jnp.arange(holders * slots, dtype=jnp.int32) // slots * capacity + position
    local = prompt_of - me * slots
    found = prompt_of[:, None] == every[None, :]
    slot_at = jnp.max(jnp.where(found, jnp.arange(holders * slots, dtype=jnp.int32)[None, :], 0), axis=1)
    block_at = jnp.max(jnp.where(found, block_of[None, :], 0), axis=1)
    same = local[:, None] == local[None, :]
    rank = jnp.sum(same & (jnp.arange(conts)[None, :] < jnp.arange(conts)[:, None]), axis=1)
    away = slot_at // slots != me
    sent_at = jnp.where(away, block_at * per + rank, -1).astype(jnp.int32)
    kept_at = jnp.where(away, -1, slot_at % slots * per + rank).astype(jnp.int32)
    slot_owner = slot_prompt // slots
    mine_before = (slot_owner[:, None] == slot_owner[None, :]) & before
    slot_block = slot_owner * capacity + jnp.sum(mine_before, axis=1)
    slot_block = jnp.where(slot_owner == me, -1, slot_block)
    served = jnp.where(
        slot_block[:, None] < 0, -1, slot_block[:, None] * per + jnp.arange(per)[None, :]
    ).reshape(-1)
    sends = jnp.arange(holders * capacity * per)

    total = 2 * hf + hd
    queries = jnp.concatenate([projected[:, :hf], projected[:, total : total + hf]], axis=1)
    outgoing = dot((sends[:, None] == sent_at[None, :]).astype(BF16), queries).astype(BF16)
    incoming = lax.all_to_all(
        outgoing.reshape(holders, capacity * per, 2 * hf), axes, split_axis=0, concat_axis=0, tiled=True
    ).reshape(-1, 2 * hf)
    acc = tail_terms(projected, tail_keys, tail_values, tail_length[:, None], heads, tail)
    kept_queries = dot((jnp.arange(conts)[:, None] == kept_at[None, :]).astype(BF16), queries)
    slot_queries = dot((served[:, None] == sends[None, :]).astype(BF16), incoming) + kept_queries
    prompt = prompt_terms(slot_queries.astype(BF16), states, heads, slots)
    back = dot((sends[:, None] == served[None, :]).astype(BF16), prompt).astype(BF16)
    answers = lax.all_to_all(
        back.reshape(holders, capacity * per, -1), axes, split_axis=0, concat_axis=0, tiled=True
    ).reshape(back.shape)
    heads_out = combine(acc, sent_at[:, None], kept_at[:, None], answers, prompt, heads)

    everyone = lax.all_gather(heads_out, "col", axis=0, tiled=True)
    terms = jnp.concatenate(
        [dot(everyone[:, t * hd : (t + 1) * hd], w_out).astype(BF16) for t in range(2)], axis=1
    )
    mixed = lax.psum_scatter(terms, "row", scatter_dimension=0, tiled=True)
    return (mixed.astype(F32) + flat.astype(F32)).astype(BF16).reshape(tokens.shape)


def solution(mesh):
    return jax.shard_map(
        body,
        mesh=mesh,
        in_specs=(
            P(("req", "row"), None, "col"),
            P("col", "row"),
            P("col", "row"),
            P("row", "col"),
            P("row", "col"),
            P(("req", "col"), None, "row"),
            P(("req", "col"), None, "row"),
            P(("req", "col")),
            P(("req", "col")),
            P(("req", "col"), "row"),
            P(("req", "col"), "row"),
            P(("req", "col")),
        ),
        out_specs=P(("req", "row"), None, "col"),
        check_vma=False,
    )
```

time: 747 us -> 377 us (0.50); the launches traced: 732 us -> 375 us
  local copies, waits for them, and re-layouts: 336 us -> 18 us
  matrix products: 111 us -> 18.6 us
  Pallas kernels: 0 us -> 73.9 us
  other arithmetic: 55.3 us -> 12.2 us
  waiting for transfers between devices: 197 us -> 218 us
  blocking collectives: 0 us -> 8.6 us
  starting transfers between devices: 19.2 us -> 11.6 us
    reshape x17 -> x4, local copies, waits for them, and re-layouts: 123 us -> 3.77 us  [the longest x2 2.96 us: body(): w_value.reshape(heads, depth, HEAD_DIM)]
    dot_general x10 -> x8, matrix products: 111 us -> 18.6 us  [dot(): return jnp.dot(a, b, preferred_element_type=F32)]
    pallas_call x0 -> x4, Pallas kernels: none -> 73.9 us  [the longest x1 26.3 us: tail_terms(): pl.pallas_call(functools.partial(tail_kernel, heads, tail), grid=(conts /...]
    transpose x2 -> x0, local copies, waits for them, and re-layouts: 35 us -> none  [the longest x1 29.2 us: body(): jnp.moveaxis(cached_state[0].reshape(taylor, local_width, prompts_here),...]
    all_gather x2, waiting for transfers between devices: 69.4 us -> 102 us  [the longest x1 53.5 us: body(): everyone = lax.all_gather(heads_out, 'col', axis=0, tiled=True)]
    gather x8 -> x0, local copies, waits for them, and re-layouts: 30.4 us -> none  [the longest x1 11.6 us: body(): pool_state[located].reshape(prompts_here, taylor, heads_here, HEAD_DIM)]
    mul x2 -> x1, local copies, waits for them, and re-layouts: 28 us -> 0.14 us  [body(): sent_at = jnp.where(away, block_at * per + rank, -1).astype(jnp.int32)]
    another operation x1 -> x0, local copies, waits for them, and re-layouts: 26.9 us -> none  [body(): cached_state[0].reshape(taylor, local_width, prompts_here)]
  transfers between devices with their start and end apart: 7 -> 6, of which waited for: 4 -> 6; matrix products, arithmetic and copies ran while one was open for 50% -> 2% of each run, Pallas kernels for 0% -> 12%
where the time goes in v1:
time: 377 us; the launch traced here: 375 us
  waiting for transfers between devices  218 us (58%)
  Pallas kernels  73.9 us (20%)
  matrix products  18.6 us (5%)
  local copies, waits for them, and re-layouts  18 us (5%)
  between operations  14.1 us (4%)
  other arithmetic  12.2 us (3%)
  starting transfers between devices  11.6 us (3%)
  blocking collectives  8.6 us (2%)
    all_gather x1, waiting for transfers between devices, body(): everyone = lax.all_gather(heads_out, 'col', axis=0, tiled=True)  53.5 us
    reduce_scatter x1, waiting for transfers between devices, body(): mixed = lax.psum_scatter(terms, 'row', scatter_dimension=0, tiled=True)  48.8 us
    all_gather x1, waiting for transfers between devices, body(): gathered = lax.all_gather(flat, 'row', axis=0, tiled=True)  48.8 us
    reduce_scatter x1, waiting for transfers between devices, body(): lax.psum_scatter(partial_sums, 'col', scatter_dimension=0, tiled=True)  47 us
    pallas_call x1, Pallas kernels, tail_terms(): pl.pallas_call(functools.partial(tail_kernel, heads, tail), grid=(conts /...  26.3 us
    pallas_call x1, Pallas kernels, turn_states(): pl.pallas_call(state_kernel, grid=(heads,), in_specs=[pl.BlockSpec((width...  19.2 us
    dot_general x8, matrix products, dot(): return jnp.dot(a, b, preferred_element_type=F32)  18.6 us
    pallas_call x1, Pallas kernels, prompt_terms(): pl.pallas_call(prompt_kernel, grid=(heads,), in_specs=[pl.BlockSpec(slot_...  17.9 us
  transfers between devices with their start and end apart: 6, of which 6 were waited for; matrix products, arithmetic and copies ran while one was open for 2% of the time, Pallas kernels for 12%

profile of v1, /device:TPU:9, one launch (start us, length us, event | category | flops | bytes accessed | tf_op | source)
XLA Modules:
  0.0 374.8 jit_solution(6133316878855939881)
XLA Ops:
  7.3 2.4 reshape.263
  12.1 48.8 %all-gather.3.cloned.1.call-done = bf16[2048,896]{0,1:T(8,128)(2,1)} async-done(((bf16[1024,896]{0,1:T(8,128)(2,1)}), bf16[2048,896]{0,1:T(8,128)(2,1)}) %all-gather.3.cloned.1.call-update) | async-done | bytes 3670032 | tf_op jit(solution)/shard_map/all_gather | solution.py:311
  60.9 4.6 %fusion = bf16[2048,1152]{1,0:T(8,128)(2,1)S(1)} fusion(bf16[448,1152]{1,0:T(8,128)(2,1)S(1)} %constant_dynamic-update-slice_fusion, bf16[2048,896]{0,1:T(8,128)(2,1)} %all-gather.3.cloned.1.call-done), kind=kOutput, calls=%fused_computation.3 | convolution fusion | flops 2116288512 | bytes 7585792 | tf_op jit(solution)/shard_map/dot_general | solution.py:22
  65.5 3.2 fusion.1
  68.8 4.7 %pad_maximum_fusion = bf16[2048,2304]{1,0:T(8,128)(2,1)} fusion(bf16[2048,1152]{1,0:T(8,128)(2,1)S(1)} %fusion.1, bf16[2048,1152]{1,0:T(8,128)(2,1)S(1)} %fusion), kind=kLoop, calls=%fused_computation | loop fusion | flops 18874368 | bytes 18874368 | tf_op jit(solution)/shard_map/concatenate | solution.py:314
  75.6 8.6 %all-reduce = s32[512]{0:T(512)S(1)} all-reduce(s32[512]{0:T(512)S(1)} %dynamic-update-slice), channel_id=1, replica_groups=mesh['req'=4,'row'=2,'col'=4] {'req','col'}, use_global_device_ids=true, to_apply=%add | all-reduce | flops 512 | bytes 4096
  85.9 19.2 %shard_map.227.states_ref = bf16[8,32,128,384]{3,2,1,0:T(8,128)(2,1)} custom-call(bf16[256,256]{1,0:T(8,128)(2,1)S(1)} %copy-done.13, bf16[1,273,28672]{2,1,0:T(8,128)(2,1)} %state_ref.1, bf16[8,32,273]{2,1,0:T(8,128)(2,1)S(1)} %bitcast.28), custom_call_target="tpu_custom_call" | custom-call | flops 20000000000 | bytes 45000000 | tf_op jit(solution)/shard_map/pallas_call | solution.py:64
  105.1 47.0 %reduce-scatter.3.cloned.1.call-done.q_ref = bf16[512,2304]{1,0:T(8,128)(2,1)} async-done(((bf16[2048,2304]{1,0:T(8,128)(2,1)}), bf16[512,2304]{1,0:T(8,128)(2,1)}) %reduce-scatter.3.cloned.1.call-update) | async-done | bytes 2359312 | tf_op jit(solution)/shard_map/reduce_scatter | solution.py:317
  154.1 5.5 %all-to-all-start = ((bf16[16,32,256]{2,1,0:T(8,128)(2,1)}), bf16[16,32,256]{2,1,0:T(8,128)(2,1)S(1)}, u32[]{:S(2)}, u32[]{:S(2)}) async-start(bf16[16,32,256]{2,1,0:T(8,128)(2,1)} %bitcast.9), calls=%async_computation.1 | async-start | bytes 524288 | tf_op jit(solution)/shard_map/all_to_all | solution.py:345
  159.8 8.5 %all-to-all-done = bf16[16,32,256]{2,1,0:T(8,128)(2,1)S(1)} async-done(((bf16[16,32,256]{2,1,0:T(8,128)(2,1)}), bf16[16,32,256]{2,1,0:T(8,128)(2,1)S(1)}, u32[]{:S(2)}, u32[]{:S(2)}) %all-to-all-start) | async-done | bytes 262176 | tf_op jit(solution)/shard_map/all_to_all | solution.py:345
  169.0 1.4 copy-done.3
  170.4 17.9 %shard_map.228.kept_ref = bf16[512,2048]{1,0:T(8,128)(2,1)S(1)} custom-call(bf16[512,256]{1,0:T(8,128)(2,1)S(1)} %fusion.14.q_ref, bf16[8,128,768]{2,1,0:T(8,128)(2,1)S(1)} %copy-done.3, f32[8,384]{1,0:T(8,128)S(1)} %copy-done.4, bf16[8,32,128,384]{3,2,1,0:T(8,128)(2,1)} %shard_map.227.states_ref), custom_call_target="tpu_custom_call" | custom-call | tf_op jit(solution)/shard_map/pallas_call | solution.py:132
  188.3 2.7 convolution_convert_fusion.2
  190.9 5.8 %all-to-all-start.1 = ((bf16[16,32,2048]{2,1,0:T(8,128)(2,1)}), bf16[16,32,2048]{2,1,0:T(8,128)(2,1)}, u32[]{:S(2)}, u32[]{:S(2)}) async-start(bf16[16,32,2048]{2,1,0:T(8,128)(2,1)} %bitcast.12), calls=%async_computation.2 | async-start | bytes 4194304 | tf_op jit(solution)/shard_map/all_to_all | solution.py:353
  198.9 1.5 copy-done.6
  206.2 26.3 %shard_map.226.acc_ref = f32[512,2048]{1,0:T(8,128)} custom-call(bf16[512,2304]{1,0:T(8,128)(2,1)} %reduce-scatter.3.cloned.1.call-done.q_ref, bf16[512,1024]{1,0:T(8,128)(2,1)S(1)} %copy-done.5, bf16[512,7168]{1,0:T(8,128)(2,1)} %tv_ref.1, s32[512,1]{1,0:T(8,128)S(1)} %copy.43.len_ref, bf16[128,1024]{1,0:T(8,128)(2,1)S(1)} %copy-done.9, ...), custom_call_target="tpu_custom_call" | custom-call | flops 20000000000 | bytes 25000000 | tf_op jit(solution)/shard_map/pallas_call | solution.py:222
  232.5 10.3 %all-to-all-done.1 = bf16[16,32,2048]{2,1,0:T(8,128)(2,1)} async-done(((bf16[16,32,2048]{2,1,0:T(8,128)(2,1)}), bf16[16,32,2048]{2,1,0:T(8,128)(2,1)}, u32[]{:S(2)}, u32[]{:S(2)}) %all-to-all-start.1) | async-done | bytes 2097184 | tf_op jit(solution)/shard_map/all_to_all | solution.py:353
  242.8 10.6 %shard_map.229 = bf16[512,1792]{1,0:T(8,128)(2,1)} custom-call(f32[512,2048]{1,0:T(8,128)} %shard_map.226.acc_ref, s32[512,1]{1,0:T(8,128)S(1)} %get-tuple-element.12.sent_at, s32[512,1]{1,0:T(8,128)S(1)} %get-tuple-element.11.kept_at, bf16[512,2048]{1,0:T(8,128)(2,1)} %bitcast.13.got_ref, bf16[512,2048]{1,0:T(8,128)(2,1)} %copy-done.1, ...), custom_call_target="tpu_custom_call" | custom-call | tf_op jit(solution)/shard_map/pallas_call | solution.py:273
  253.8 53.5 %all-gather.5.cloned.1.call-done = bf16[2048,1792]{1,0:T(8,128)(2,1)} async-done(((bf16[512,1792]{1,0:T(8,128)(2,1)}), bf16[2048,1792]{1,0:T(8,128)(2,1)}) %all-gather.5.cloned.1.call-update) | async-done | bytes 7340048 | tf_op jit(solution)/shard_map/all_gather | solution.py:358
  307.3 4.3 %fusion.6 = bf16[2048,448]{0,1:T(8,128)(2,1)S(1)} fusion(bf16[896,448]{0,1:T(8,128)(2,1)S(1)} %copy-done, bf16[2048,1792]{1,0:T(8,128)(2,1)} %all-gather.5.cloned.1.call-done), kind=kOutput, calls=%fused_computation.12 | convolution fusion | flops 1645084672 | bytes 6307840 | tf_op jit(solution)/shard_map/dot_general | solution.py:22
  311.5 2.1 fusion.9
  313.7 2.2 pad_maximum_fusion.1
  315.9 48.8 %reduce-scatter.5.cloned.1.call-done = bf16[1024,896]{0,1:T(8,128)(2,1)} async-done(((bf16[2048,896]{0,1:T(8,128)(2,1)}), bf16[1024,896]{0,1:T(8,128)(2,1)}) %reduce-scatter.5.cloned.1.call-update) | async-done | bytes 1835024 | tf_op jit(solution)/shard_map/reduce_scatter | solution.py:362
  364.8 3.5 add_convert_fusion
  (88 shorter events, 17.3 us)
Async XLA Ops:
  6.5 300.7 %copy-start = (bf16[896,448]{0,1:T(8,128)(2,1)S(1)}, bf16[896,448]{0,1:T(8,128)(2,1)}, u32[]{:S(2)}) copy-start(bf16[896,448]{0,1:T(8,128)(2,1)} %param.28) | copy-start | bytes 2408452
  6.5 4.5 %copy-start.17 = (bf16[448,128]{1,0:T(8,128)(2,1)S(1)}, bf16[448,128]{1,0:T(8,128)(2,1)}, u32[]{:S(2)}) copy-start(bf16[448,128]{1,0:T(8,128)(2,1)} %param.25) | copy-start | bytes 344068
  6.5 54.4 %all-gather.3.cloned.1.call-start = ((), (), s32[]{:S(2)}) async-start(), calls=%async_computation.4 | async-start | bytes 5505024 | tf_op jit(solution)/shard_map/all_gather | solution.py:311
  7.3 144.8 %reduce-scatter.3.cloned.1.call-start = ((), (), s32[]{:S(2)}) async-start(), calls=%async_computation.5 | async-start | bytes 11796480 | tf_op jit(solution)/shard_map/reduce_scatter | solution.py:317
  60.9 4.6 %copy-start.22 = (bf16[2048,896]{0,1:T(8,128)(2,1)S(1)}, bf16[2048,896]{0,1:T(8,128)(2,1)}, u32[]{:S(2)}) copy-start(bf16[2048,896]{0,1:T(8,128)(2,1)} %all-gather.3.cloned.1.call-done) | copy-start | bytes 11010052
  73.5 1.9 copy-start.20
  73.5 11.4 %copy-start.16 = (bf16[32,273,8]{1,2,0:T(8,128)(2,1)S(1)}, bf16[32,273,8]{1,2,0:T(8,128)(2,1)}, u32[]{:S(2)}) copy-start(bf16[32,273,8]{1,2,0:T(8,128)(2,1)} %param.30) | copy-start | bytes 419332
  73.5 11.6 %copy-start.18 = (s32[512]{0:T(512)S(1)}, s32[512]{0:T(512)}, u32[]{:S(2)}) copy-start(s32[512]{0:T(512)} %param.32) | copy-start | bytes 6148
  73.5 12.4 %copy-start.13 = (bf16[256,256]{1,0:T(8,128)(2,1)S(1)}, bf16[256,256]{1,0:T(8,128)(2,1)}, u32[]{:S(2)}) copy-start(bf16[256,256]{1,0:T(8,128)(2,1)} %constant.99.clone.perm_ref) | copy-start | bytes 393220
  105.1 63.9 %copy-start.4 = (f32[8,384]{1,0:T(8,128)S(1)}, f32[8,384]{1,0:T(8,128)}, u32[]{:S(2)}) copy-start(f32[8,384]{1,0:T(8,128)} %constant.109.clone.shift_ref) | copy-start | bytes 36868
  154.1 14.2 %all-to-all-start = ((bf16[16,32,256]{2,1,0:T(8,128)(2,1)}), bf16[16,32,256]{2,1,0:T(8,128)(2,1)S(1)}, u32[]{:S(2)}, u32[]{:S(2)}) async-start(bf16[16,32,256]{2,1,0:T(8,128)(2,1)} %bitcast.9), calls=%async_computation.1 | async-start | bytes 524288 | tf_op jit(solution)/shard_map/all_to_all | solution.py:345
  169.0 1.4 copy-start.3
  188.2 2.7 copy-start.1
  190.9 6.3 %copy-start.19 = (s32[512]{0:T(512)S(1)}, s32[512]{0:T(512)}, u32[]{:S(2)}) copy-start(s32[512]{0:T(512)} %param.35) | copy-start | bytes 6148
  190.9 6.8 %copy-start.12 = (bf16[64,1024]{1,0:T(8,128)(2,1)S(1)}, bf16[64,1024]{1,0:T(8,128)(2,1)}, u32[]{:S(2)}) copy-start(bf16[64,1024]{1,0:T(8,128)(2,1)} %constant.104.clone.dw) | copy-start | bytes 393220
  190.9 51.9 %all-to-all-start.1 = ((bf16[16,32,2048]{2,1,0:T(8,128)(2,1)}), bf16[16,32,2048]{2,1,0:T(8,128)(2,1)}, u32[]{:S(2)}, u32[]{:S(2)}) async-start(bf16[16,32,2048]{2,1,0:T(8,128)(2,1)} %bitcast.12), calls=%async_computation.2 | async-start | bytes 4194304 | tf_op jit(solution)/shard_map/all_to_all | solution.py:353
  196.7 110.5 %all-gather.5.cloned.1.call-start = ((), (), s32[]{:S(2)}) async-start(), calls=%async_computation.6 | async-start | bytes 9175040 | tf_op jit(solution)/shard_map/all_gather | solution.py:358
  197.7 1.2 copy-start.5
  198.9 1.5 copy-start.6
  200.4 1.2 copy-start.7
  206.2 36.6 %copy-start.2 = (bf16[1024,896]{1,0:T(8,128)(2,1)S(1)}, bf16[1024,896]{1,0:T(8,128)(2,1)}, u32[]{:S(2)}) copy-start(bf16[1024,896]{1,0:T(8,128)(2,1)} %constant.110.clone.pack) | copy-start | bytes 5505028
  253.5 111.3 %reduce-scatter.5.cloned.1.call-start = ((), (), s32[]{:S(2)}) async-start(), calls=%async_computation.7 | async-start | bytes 5505024 | tf_op jit(solution)/shard_map/reduce_scatter | solution.py:362
  307.3 4.3 %copy-start.21 = (bf16[2048,1792]{1,0:T(8,128)(2,1)S(1)}, bf16[2048,1792]{1,0:T(8,128)(2,1)}, u32[]{:S(2)}) copy-start(bf16[2048,1792]{1,0:T(8,128)(2,1)} %all-gather.5.cloned.1.call-done) | copy-start | bytes 22020100
  315.9 48.9 %copy-start.15 = (bf16[1024,2,448]{0,2,1:T(8,128)(2,1)S(1)}, bf16[1024,2,448]{0,2,1:T(8,128)(2,1)}, u32[]{:S(2)}) copy-start(bf16[1024,2,448]{0,2,1:T(8,128)(2,1)} %param.24) | copy-start | bytes 5505028
  (6 other events, 5.3 us)
Sparse Core Ops, SparseCore 0:
  8.9 51.9 all-gather.2
  73.6 78.4 reduce-scatter.2
  253.6 53.5 all-gather.4
  316.0 48.6 reduce-scatter.4

commit v2 on v1

--- a/solution.py
+++ b/solution.py
@@ -280,6 +280,286 @@
     )(acc, sent_at, kept_at, got, kept, pack)
 
 
+def remote(src, dst, send, recv, **target):
+    return pltpu.make_async_remote_copy(
+        src_ref=src,
+        dst_ref=dst,
+        send_sem=send,
+        recv_sem=recv,
+        device_id=target,
+        device_id_type=pl.DeviceIdType.MESH,
+    )
+
+
+def greet(targets):
+    barrier = pltpu.get_barrier_semaphore()
+    for target in targets:
+        pl.semaphore_signal(barrier, inc=1, device_id=target, device_id_type=pl.DeviceIdType.MESH)
+    pl.semaphore_wait(barrier, len(targets))
+
+
+def places():
+    row, col = lax.axis_index("row"), lax.axis_index("col")
+    across = lax.rem(col + 2, 4)
+    core = lax.rem(col, 2)
+    sibling = col + 1 - 2 * core
+    return row, 1 - row, col, across, core, sibling
+
+
+def front_kernel(
+    x, w, wo, tok, wall, woall, via, y_send, y_recv, c_send, c_recv, w_send, w_recv, o_send, o_recv, l_sem
+):
+    row, partner, col, across, core, sibling = places()
+    greet([{"row": partner}] + [{"col": lax.rem(col + k, 4)} for k in (1, 2, 3)])
+    size = tok.shape[1] // 2
+
+    def to_row(j):
+        rows = pl.ds(j * size, size)
+        return remote(x.at[rows], via.at[rows], y_send.at[j], y_recv.at[j], row=partner)
+
+    def holder_of(source, j):
+        return 2 * (row if source == 0 else partner) + j // 2
+
+    def ends(source, j):
+        src = (x if source == 0 else via).at[pl.ds(j * size, size)]
+        return src, tok.at[col, pl.ds((j % 2) * size, size)], c_recv.at[col, j % 2]
+
+    def to_holder(source, j):
+        src, dst, arrival = ends(source, j)
+        return remote(src, dst, c_send.at[source * 4 + j], arrival, col=holder_of(source, j))
+
+    def start_holder(source, j):
+        @pl.when(holder_of(source, j) != col)
+        def _():
+            to_holder(source, j).start()
+
+        @pl.when(holder_of(source, j) == col)
+        def _():
+            pltpu.make_async_copy(*ends(source, j)).start()
+
+    for j in range(4):
+        to_row(j).start()
+    w_across = remote(w, wall.at[col], w_send.at[0], w_recv.at[0], col=across)
+    w_side = remote(w, wall.at[col], w_send.at[1], w_recv.at[1], col=sibling)
+    w_here = pltpu.make_async_copy(w, wall.at[col], l_sem.at[0])
+    o_there = remote(wo, woall.at[row], o_send, o_recv, row=partner)
+    o_here = pltpu.make_async_copy(wo, woall.at[row], l_sem.at[1])
+    for j in range(4):
+        start_holder(0, j)
+    w_across.start()
+    w_side.start()
+    w_here.start()
+    o_here.start()
+    for j in range(4):
+        to_row(j).wait_recv()
+        start_holder(1, j)
+    o_there.start()
+    w_across.wait_recv()
+    w_on = remote(wall.at[across], wall.at[across], w_send.at[2], w_recv.at[2], col=sibling)
+    w_on.start()
+    for source in range(2):
+        for j in range(4):
+
+            @pl.when(holder_of(source, j) != col)
+            def _():
+                to_holder(source, j).wait_send()
+
+    for k in range(4):
+        for part in range(2):
+            rows = pl.ds(part * size, size)
+
+            @pl.when(col != k)
+            def _():
+                remote(
+                    tok.at[k, rows], tok.at[k, rows], c_send.at[0], c_recv.at[k, part], col=across
+                ).wait_recv()
+
+            @pl.when(col == k)
+            def _():
+                pltpu.make_async_copy(tok.at[k, rows], tok.at[k, rows], c_recv.at[k, part]).wait()
+
+    for j in range(4):
+        to_row(j).wait_send()
+    w_across.wait_send()
+    w_side.wait()
+    w_on.wait()
+    w_here.wait()
+    o_there.wait()
+    o_here.wait()
+
+
+def front(x, w, wo, conts):
+    dma = pltpu.SemaphoreType.DMA
+    return pl.pallas_call(
+        front_kernel,
+        in_specs=[pl.BlockSpec(memory_space=pl.ANY)] * 3,
+        out_specs=[pl.BlockSpec(memory_space=pl.ANY)] * 4,
+        out_shape=[
+            jax.ShapeDtypeStruct((4, conts, x.shape[1]), BF16),
+            jax.ShapeDtypeStruct((4,) + w.shape, BF16),
+            jax.ShapeDtypeStruct((2,) + wo.shape, BF16),
+            jax.ShapeDtypeStruct(x.shape, BF16),
+        ],
+        scratch_shapes=[
+            dma((4,)), dma((4,)), dma((8,)), dma((4, 2)), dma((3,)), dma((3,)), dma, dma, dma((2,)),
+        ],
+        compiler_params=pltpu.CompilerParams(collective_id=0, has_side_effects=True),
+    )(x, w, wo)
+
+
+def back_kernel(h, hall, via, sx, rx, sy, ry, ss, rs, sf, rf, sl):
+    row, partner, col, across, core, sibling = places()
+    greet([{"row": partner}, {"col": across}, {"col": sibling}])
+    pieces = 4
+    size = h.shape[0] // pieces
+    stays = col // 2 == row
+
+    def at(ref, j):
+        return ref.at[pl.ds(j * size, size)]
+
+    def slot(b, half, j):
+        return hall.at[b, half, pl.ds(j * size, size)]
+
+    def x_via(j):
+        return remote(at(h, j), at(via, j), sx.at[j], rx.at[j], col=across)
+
+    def x_final(j):
+        return remote(at(h, j), slot(core, row, j), sx.at[j], rx.at[j], col=across)
+
+    def y_own(j):
+        return remote(at(h, j), slot(core, row, j), sy.at[j], ry.at[j], row=partner)
+
+    def y_via(j):
+        return remote(at(via, j), slot(core, row, j), sy.at[j], ry.at[j], row=partner)
+
+    def side_own(j):
+        return remote(at(h, j), slot(core, row, j), ss.at[j], rs.at[j], col=sibling)
+
+    def side_got(j):
+        return remote(slot(core, row, j), slot(core, row, j), ss.at[j], rs.at[j], col=sibling)
+
+    def side_far(j):
+        return remote(slot(core, partner, j), slot(core, partner, j), sf.at[j], rf.at[j], col=sibling)
+
+    def keep(j):
+        return pltpu.make_async_copy(at(h, j), slot(core, row, j), sl.at[j])
+
+    for j in range(pieces):
+
+        @pl.when(stays)
+        def _():
+            x_final(j).start()
+            side_own(j).start()
+            keep(j).start()
+
+        @pl.when(jnp.logical_not(stays))
+        def _():
+            x_via(j).start()
+            y_own(j).start()
+
+    for j in range(pieces):
+
+        @pl.when(stays)
+        def _():
+            x_via(j).wait_recv()
+            y_via(j).start()
+
+        @pl.when(jnp.logical_not(stays))
+        def _():
+            remote(slot(core, row, j), slot(core, row, j), sx.at[j], rx.at[j], col=across).wait_recv()
+            side_got(j).start()
+
+    for j in range(pieces):
+        remote(slot(core, partner, j), slot(core, partner, j), sy.at[j], ry.at[j], row=partner).wait_recv()
+        side_far(j).start()
+    for j in range(pieces):
+        near = slot(1 - core, row, j)
+        far = slot(1 - core, partner, j)
+        remote(near, near, ss.at[j], rs.at[j], col=sibling).wait_recv()
+        remote(far, far, sf.at[j], rf.at[j], col=sibling).wait_recv()
+        side_far(j).wait_send()
+
+        @pl.when(stays)
+        def _():
+            x_final(j).wait_send()
+            y_via(j).wait_send()
+            side_own(j).wait_send()
+            keep(j).wait()
+
+        @pl.when(jnp.logical_not(stays))
+        def _():
+            x_via(j).wait_send()
+            y_own(j).wait_send()
+            side_got(j).wait_send()
+
+
+def back(h):
+    dma = pltpu.SemaphoreType.DMA((4,))
+    return pl.pallas_call(
+        back_kernel,
+        in_specs=[pl.BlockSpec(memory_space=pl.ANY)],
+        out_specs=[pl.BlockSpec(memory_space=pl.ANY)] * 2,
+        out_shape=[
+            jax.ShapeDtypeStruct((2, 2) + h.shape, BF16),
+            jax.ShapeDtypeStruct(h.shape, BF16),
+        ],
+        scratch_shapes=[dma] * 9,
+        compiler_params=pltpu.CompilerParams(collective_id=1, has_side_effects=True),
+    )(h)[0]
+
+
+def project_kernel(tok_ref, w_ref, out_ref):
+    depth, total = w_ref.shape[1:]
+    for t in range(2):
+        acc = jnp.zeros((tok_ref.shape[1], total), F32)
+        for k in range(w_ref.shape[0]):
+            acc = acc + dot(tok_ref[k, :, t * depth : (t + 1) * depth], w_ref[k])
+        out_ref[:, t * total : (t + 1) * total] = acc.astype(BF16)
+
+
+def project(tok, w):
+    conts, total = tok.shape[1], w.shape[2]
+    block = 128
+    return pl.pallas_call(
+        project_kernel,
+        grid=(conts // block,),
+        in_specs=[
+            pl.BlockSpec((tok.shape[0], block, tok.shape[2]), lambda i: (0, i, 0)),
+            pl.BlockSpec(w.shape, lambda i: (0, 0, 0)),
+        ],
+        out_specs=pl.BlockSpec((block, 2 * total), lambda i: (i, 0)),
+        out_shape=jax.ShapeDtypeStruct((conts, 2 * total), BF16),
+        compiler_params=pltpu.CompilerParams(vmem_limit_bytes=VMEM_LIMIT),
+    )(tok, w)
+
+
+def output_kernel(h_ref, w_ref, x_ref, out_ref):
+    hd, depth = w_ref.shape[1:]
+    for t in range(2):
+        acc = x_ref[:, t * depth : (t + 1) * depth].astype(F32)
+        for half in range(2):
+            part = dot(h_ref[0, half, :, t * hd : (t + 1) * hd], w_ref[half])
+            acc = acc + part.astype(BF16).astype(F32)
+        out_ref[:, t * depth : (t + 1) * depth] = acc.astype(BF16)
+
+
+def output(hall, w, flat):
+    block = 128
+    steps = hall.shape[2] // block
+    return pl.pallas_call(
+        output_kernel,
+        grid=(2, steps),
+        in_specs=[
+            pl.BlockSpec((1, 2, block, hall.shape[3]), lambda b, i: (b, 0, i, 0)),
+            pl.BlockSpec(w.shape, lambda b, i: (0, 0, 0)),
+            pl.BlockSpec((block, flat.shape[1]), lambda b, i: (b * steps + i, 0)),
+        ],
+        out_specs=pl.BlockSpec((block, flat.shape[1]), lambda b, i: (b * steps + i, 0)),
+        out_shape=jax.ShapeDtypeStruct(flat.shape, BF16),
+        compiler_params=pltpu.CompilerParams(vmem_limit_bytes=VMEM_LIMIT),
+    )(hall, w, flat)
+
+
 def body(
     tokens,
     w_query,
@@ -306,15 +586,26 @@
     capacity = (slots // 2 + holders - 2) // (holders - 1)
     me = lax.axis_index(axes)
 
-    every = lax.all_gather(slot_prompt, axes, axis=0, tiled=True)
+    pair = jnp.stack([slot_prompt // slots, slot_prompt % slots]).astype(BF16)
+    pair = jnp.zeros((16, LANES), BF16).at[:2, :slots].set(pair)
+    pairs = lax.all_gather(pair, axes, axis=0, tiled=True).reshape(holders, 16, LANES)[:, :2, :slots]
+    pairs = pairs.astype(jnp.int32)
+    every = (pairs[:, 0] * slots + pairs[:, 1]).reshape(-1)
     flat = tokens.reshape(tokens.shape[0], 2 * depth)
-    gathered = lax.all_gather(flat, "row", axis=0, tiled=True)
     value_weight = jnp.moveaxis(w_value.reshape(heads, depth, HEAD_DIM), 0, 1).reshape(depth, hd)
     stacked = jnp.concatenate([w_query, w_key, value_weight], axis=1)
-    partial_sums = jnp.concatenate(
-        [dot(gathered[:, t * depth : (t + 1) * depth], stacked).astype(BF16) for t in range(2)], axis=1
-    )
-    projected = lax.psum_scatter(partial_sums, "col", scatter_dimension=0, tiled=True)
+    direct = lax.axis_size("row") == 2 and lax.axis_size("col") == 4
+    if direct:
+        tok, w_all, wo_all, _ = front(flat, stacked, w_out, conts)
+        projected = project(tok, w_all)
+    else:
+        gathered = lax.all_gather(flat, "row", axis=0, tiled=True)
+        partial_sums = [
+            dot(gathered[:, t * depth : (t + 1) * depth], stacked).astype(BF16) for t in range(2)
+        ]
+        projected = lax.psum_scatter(
+            jnp.concatenate(partial_sums, axis=1), "col", scatter_dimension=0, tiled=True
+        )
     states = turn_states(cached_state, jnp.transpose(cached_norm, (2, 0, 1)), heads, slots)
 
     owner = (every // slots).reshape(holders, slots)
@@ -349,12 +640,14 @@
     kept_queries = dot((jnp.arange(conts)[:, None] == kept_at[None, :]).astype(BF16), queries)
     slot_queries = dot((served[:, None] == sends[None, :]).astype(BF16), incoming) + kept_queries
     prompt = prompt_terms(slot_queries.astype(BF16), states, heads, slots)
-    back = dot((sends[:, None] == served[None, :]).astype(BF16), prompt).astype(BF16)
+    replies = dot((sends[:, None] == served[None, :]).astype(BF16), prompt).astype(BF16)
     answers = lax.all_to_all(
-        back.reshape(holders, capacity * per, -1), axes, split_axis=0, concat_axis=0, tiled=True
-    ).reshape(back.shape)
+        replies.reshape(holders, capacity * per, -1), axes, split_axis=0, concat_axis=0, tiled=True
+    ).reshape(replies.shape)
     heads_out = combine(acc, sent_at[:, None], kept_at[:, None], answers, prompt, heads)
 
+    if direct:
+        return output(back(heads_out), wo_all, flat).reshape(tokens.shape)
     everyone = lax.all_gather(heads_out, "col", axis=0, tiled=True)
     terms = jnp.concatenate(
         [dot(everyone[:, t * hd : (t + 1) * hd], w_out).astype(BF16) for t in range(2)], axis=1

time: 377 us -> 321 us (0.85)
  waiting for transfers between devices: 218 us -> 10.4 us
  Pallas kernels: 73.9 us -> 239 us
  matrix products: 18.6 us -> 4.39 us
  between operations: 14.1 us -> 0.4 us
  blocking collectives: 8.6 us -> 19.5 us
  local copies, waits for them, and re-layouts: 18 us -> 28.4 us
  other arithmetic: 12.2 us -> 4.2 us
    pallas_call x0 -> x4, Pallas kernels: none -> 167 us  [the longest x1 89.5 us: front(): pl.pallas_call(front_kernel, in_specs=[pl.BlockSpec(memory_space=pl.ANY)]...]
    all_gather x2 -> x0, waiting for transfers between devices: 102 us -> none  [the longest x1 53.5 us: body(): everyone = lax.all_gather(heads_out, 'col', axis=0, tiled=True)]
    reduce_scatter x2 -> x0, waiting for transfers between devices: 95.9 us -> none  [the longest x1 48.8 us: body(): mixed = lax.psum_scatter(terms, 'row', scatter_dimension=0, tiled=True)]
    all_gather x0 -> x1, blocking collectives: none -> 19.5 us  [body(): lax.all_gather(pair, axes, axis=0, tiled=True).reshape(holders, 16, LANES)]
    dot_general x8 -> x4, matrix products: 18.6 us -> 4.39 us  [dot(): return jnp.dot(a, b, preferred_element_type=F32)]
    unnamed x1 -> x0, blocking collectives: 8.6 us -> none
    all_to_all x1, waiting for transfers between devices: 8.5 us -> 0.01 us  [body(): lax.all_to_all(outgoing.reshape(holders, capacity * per, 2 * hf), axes, s...]
    concatenate x2 -> x1, other arithmetic: 6.9 us -> 1.09 us  [body(): stacked = jnp.concatenate([w_query, w_key, value_weight], axis=1)]
  transfers between devices with their start and end apart: 6 -> 2, of which waited for: 6 -> 1; matrix products, arithmetic and copies ran while one was open for 2% -> 0% of each run, Pallas kernels for 12% -> 14%
where the time goes in v2:
time: 321 us; the launch traced here: 319 us
  Pallas kernels  239 us (74%)
  local copies, waits for them, and re-layouts  28.4 us (9%)
  blocking collectives  19.5 us (6%)
  starting transfers between devices  12.9 us (4%)
  waiting for transfers between devices  10.4 us (3%)
  matrix products  4.39 us (1%)
  other arithmetic  4.2 us (1%)
    pallas_call x1, Pallas kernels, front(): pl.pallas_call(front_kernel, in_specs=[pl.BlockSpec(memory_space=pl.ANY)]...  89.5 us
    pallas_call x1, Pallas kernels, back(): pl.pallas_call(back_kernel, in_specs=[pl.BlockSpec(memory_space=pl.ANY)],...  59.6 us
    pallas_call x1, Pallas kernels, tail_terms(): pl.pallas_call(functools.partial(tail_kernel, heads, tail), grid=(conts /...  26.3 us
    all_gather x1, blocking collectives, body(): lax.all_gather(pair, axes, axis=0, tiled=True).reshape(holders, 16, LANES)  19.5 us
    pallas_call x1, Pallas kernels, turn_states(): pl.pallas_call(state_kernel, grid=(heads,), in_specs=[pl.BlockSpec((width...  18.5 us
    pallas_call x1, Pallas kernels, prompt_terms(): pl.pallas_call(prompt_kernel, grid=(heads,), in_specs=[pl.BlockSpec(slot_...  17.9 us
    unnamed x56, local copies, waits for them, and re-layouts  16.8 us
    all_to_all x1, waiting for transfers between devices, body(): lax.all_to_all(replies.reshape(holders, capacity * per, -1), axes, split_...  10.4 us
  transfers between devices with their start and end apart: 2, of which 1 were waited for; matrix products, arithmetic and copies ran while one was open for 0% of the time, Pallas kernels for 14%

profile of v2, /device:TPU:9, one launch (start us, length us, event | category | flops | bytes accessed | tf_op | source)
XLA Modules:
  0.0 319.4 jit_solution(8570791426956239801)
XLA Ops:
  0.8 19.5 %all_gather.3 = bf16[256,128]{1,0:T(8,128)(2,1)S(1)} all-gather(bf16[16,128]{1,0:T(8,128)(2,1)S(1)} %fusion.22), channel_id=1, replica_groups=mesh['req'=4,'row'=2,'col'=4] {'req','col'}, dimensions={0}, use_global_device_ids=true | all-gather | bytes 69632 | tf_op jit(solution)/shard_map/all_gather | solution.py:591
  22.2 3.8 %copy.45.x.x_ref = bf16[1024,896]{1,0:T(8,128)(2,1)} copy(bf16[1024,896]{0,1:T(8,128)(2,1)} %bitcast.27) | data formatting | bytes 3670016 | tf_op jit(solution)/shard_map/reshape | solution.py:594
  26.0 1.3 reshape.339
  28.7 1.5 copy.46.wo
  30.2 1.1 pad_maximum_fusion.w
  31.3 89.5 %shard_map.226 = (bf16[4,512,896]{2,1,0:T(8,128)(2,1)}, bf16[4,448,1152]{2,1,0:T(8,128)(2,1)}, bf16[2,896,448]{2,1,0:T(8,128)(2,1)}, bf16[1024,896]{1,0:T(8,128)(2,1)}) custom-call(bf16[1024,896]{1,0:T(8,128)(2,1)} %copy.45.x.x_ref, bf16[448,1152]{1,0:T(8,128)(2,1)} %pad_maximum_fusion.w, bf16[896,448]{1,0:T(8,128)(2,1)} %copy.46.wo), custom_call_target="tpu_custom_call" | custom-call | tf_op jit(solution)/shard_map/pallas_call | solution.py:393
  120.8 2.0 copy-done.4
  122.9 8.6 %shard_map.227.q_ref = bf16[512,2304]{1,0:T(8,128)(2,1)S(1)} custom-call(bf16[4,512,896]{2,1,0:T(8,128)(2,1)S(1)} %copy-done.4, bf16[4,448,1152]{2,1,0:T(8,128)(2,1)} %get-tuple-element.22.w_ref), custom_call_target="tpu_custom_call" | custom-call | tf_op jit(solution)/shard_map/pallas_call | solution.py:523
  133.2 6.7 %all-to-all-start = ((bf16[16,32,256]{2,1,0:T(8,128)(2,1)}), bf16[16,32,256]{2,1,0:T(8,128)(2,1)S(1)}, u32[]{:S(2)}, u32[]{:S(2)}) async-start(bf16[16,32,256]{2,1,0:T(8,128)(2,1)} %bitcast.11), calls=%async_computation | async-start | bytes 524288 | tf_op jit(solution)/shard_map/all_to_all | solution.py:636
  140.1 18.5 %shard_map.229.states_ref = bf16[8,32,128,384]{3,2,1,0:T(8,128)(2,1)} custom-call(bf16[256,256]{1,0:T(8,128)(2,1)S(1)} %copy-done.18, bf16[1,273,28672]{2,1,0:T(8,128)(2,1)} %state_ref.1, bf16[8,32,273]{2,1,0:T(8,128)(2,1)S(1)} %bitcast.25), custom_call_target="tpu_custom_call" | custom-call | flops 20000000000 | bytes 45000000 | tf_op jit(solution)/shard_map/pallas_call | solution.py:64
  160.1 17.9 %shard_map.230.kept_ref = bf16[512,2048]{1,0:T(8,128)(2,1)S(1)} custom-call(bf16[512,256]{1,0:T(8,128)(2,1)S(1)} %fusion.q_ref, bf16[8,128,768]{2,1,0:T(8,128)(2,1)S(1)} %copy-done.8, f32[8,384]{1,0:T(8,128)S(1)} %copy-done.9, bf16[8,32,128,384]{3,2,1,0:T(8,128)(2,1)} %shard_map.229.states_ref), custom_call_target="tpu_custom_call" | custom-call | tf_op jit(solution)/shard_map/pallas_call | solution.py:132
  178.0 2.7 convolution_convert_fusion
  180.6 6.2 %all-to-all-start.1 = ((bf16[16,32,2048]{2,1,0:T(8,128)(2,1)}), bf16[16,32,2048]{2,1,0:T(8,128)(2,1)}, u32[]{:S(2)}, u32[]{:S(2)}) async-start(bf16[16,32,2048]{2,1,0:T(8,128)(2,1)} %bitcast.14), calls=%async_computation.1 | async-start | bytes 4194304 | tf_op jit(solution)/shard_map/all_to_all | solution.py:644
  188.0 1.2 copy-done.10
  189.3 1.5 copy-done.11
  196.3 26.3 %shard_map.228.acc_ref = f32[512,2048]{1,0:T(8,128)} custom-call(bf16[512,2304]{1,0:T(8,128)(2,1)} %copy-done.5, bf16[512,1024]{1,0:T(8,128)(2,1)S(1)} %copy-done.10, bf16[512,7168]{1,0:T(8,128)(2,1)} %tv_ref.1, s32[512,1]{1,0:T(8,128)S(1)} %copy.47.len_ref, bf16[128,1024]{1,0:T(8,128)(2,1)S(1)} %copy-done.14, bf16[1024,64]{1,0:T(8,128)(2,1)S(1)} %copy-done.15, ...), custom_call_target="tpu_custom_call" | custom-call | flops 20000000000 | bytes 25000000 | tf_op jit(solution)/shard_map/pallas_call | solution.py:222
  222.6 10.4 %all-to-all-done.1 = bf16[16,32,2048]{2,1,0:T(8,128)(2,1)} async-done(((bf16[16,32,2048]{2,1,0:T(8,128)(2,1)}), bf16[16,32,2048]{2,1,0:T(8,128)(2,1)}, u32[]{:S(2)}, u32[]{:S(2)}) %all-to-all-start.1) | async-done | bytes 2097184 | tf_op jit(solution)/shard_map/all_to_all | solution.py:644
  232.9 9.9 %shard_map.231.h = bf16[512,1792]{1,0:T(8,128)(2,1)S(1)} custom-call(f32[512,2048]{1,0:T(8,128)} %shard_map.228.acc_ref, s32[512,1]{1,0:T(8,128)S(1)} %get-tuple-element.36.sent_at, s32[512,1]{1,0:T(8,128)S(1)} %get-tuple-element.35.kept_at, bf16[512,2048]{1,0:T(8,128)(2,1)} %bitcast.15.got_ref, bf16[512,2048]{1,0:T(8,128)(2,1)} %copy-done.1, ...), custom_call_target="tpu_custom_call" | custom-call | tf_op jit(solution)/shard_map/pallas_call | solution.py:273
  242.9 1.3 copy-done.2
  244.2 59.6 %shard_map.232 = (bf16[2,2,512,1792]{3,2,1,0:T(8,128)(2,1)}, bf16[512,1792]{1,0:T(8,128)(2,1)}) custom-call(bf16[512,1792]{1,0:T(8,128)(2,1)} %copy-done.2), custom_call_target="tpu_custom_call" | custom-call | tf_op jit(solution)/shard_map/pallas_call | solution.py:498
  303.8 1.5 copy-done.7
  305.3 9.0 %shard_map.233 = bf16[1024,896]{1,0:T(8,128)(2,1)S(1)} custom-call(bf16[2,2,512,1792]{3,2,1,0:T(8,128)(2,1)} %get-tuple-element.23.h_ref, bf16[2,896,448]{2,1,0:T(8,128)(2,1)S(1)} %copy-done.7, bf16[1024,896]{1,0:T(8,128)(2,1)S(1)} %copy-done), custom_call_target="tpu_custom_call" | custom-call | tf_op jit(solution)/shard_map/pallas_call | solution.py:549
  314.3 1.3 copy-done.3
  315.6 3.8 %copy.57 = bf16[1024,896]{0,1:T(8,128)(2,1)} copy(bf16[1024,896]{1,0:T(8,128)(2,1)} %copy-done.3) | data formatting | bytes 3670016 | tf_op jit(solution)/shard_map/pallas_call | solution.py:549
  (81 shorter events, 14.0 us)
Async XLA Ops:
  0.0 26.0 %copy-start.20 = (bf16[8,50176]{1,0:T(8,128)(2,1)S(1)}, bf16[8,50176]{1,0:T(8,128)(2,1)}, u32[]{:S(2)}) copy-start(bf16[8,50176]{1,0:T(8,128)(2,1)} %param.29) | copy-start | bytes 2408452
  27.3 1.4 copy-start.21
  27.9 2.3 copy-start.23
  27.9 2.3 copy-start.24
  120.8 2.0 copy-start.4
  122.9 8.7 %copy-start.25 = (s32[512]{0:T(512)S(1)}, s32[512]{0:T(512)}, u32[]{:S(2)}) copy-start(s32[512]{0:T(512)} %param.34) | copy-start | bytes 6148
  131.5 27.2 %copy-start.5 = (bf16[512,2304]{1,0:T(8,128)(2,1)}, bf16[512,2304]{1,0:T(8,128)(2,1)S(1)}, u32[]{:S(2)}) copy-start(bf16[512,2304]{1,0:T(8,128)(2,1)S(1)} %shard_map.227.q_ref) | copy-start | bytes 7077892
  131.5 8.6 %copy-start.22 = (bf16[32,273,8]{1,2,0:T(8,128)(2,1)S(1)}, bf16[32,273,8]{1,2,0:T(8,128)(2,1)}, u32[]{:S(2)}) copy-start(bf16[32,273,8]{1,2,0:T(8,128)(2,1)} %param.32) | copy-start | bytes 419332
  131.5 8.6 %copy-start.18 = (bf16[256,256]{1,0:T(8,128)(2,1)S(1)}, bf16[256,256]{1,0:T(8,128)(2,1)}, u32[]{:S(2)}) copy-start(bf16[256,256]{1,0:T(8,128)(2,1)} %constant.137.clone.perm_ref) | copy-start | bytes 393220
  133.2 25.6 %all-to-all-start = ((bf16[16,32,256]{2,1,0:T(8,128)(2,1)}), bf16[16,32,256]{2,1,0:T(8,128)(2,1)S(1)}, u32[]{:S(2)}, u32[]{:S(2)}) async-start(bf16[16,32,256]{2,1,0:T(8,128)(2,1)} %bitcast.11), calls=%async_computation | async-start | bytes 524288 | tf_op jit(solution)/shard_map/all_to_all | solution.py:636
  140.1 19.4 %copy-start.9 = (f32[8,384]{1,0:T(8,128)S(1)}, f32[8,384]{1,0:T(8,128)}, u32[]{:S(2)}) copy-start(f32[8,384]{1,0:T(8,128)} %constant.147.clone.shift_ref) | copy-start | bytes 36868
  158.7 1.4 copy-start.8
  178.0 2.7 copy-start.1
  180.6 6.7 %copy-start.26 = (s32[512]{0:T(512)S(1)}, s32[512]{0:T(512)}, u32[]{:S(2)}) copy-start(s32[512]{0:T(512)} %param.37) | copy-start | bytes 6148
  180.6 52.3 %all-to-all-start.1 = ((bf16[16,32,2048]{2,1,0:T(8,128)(2,1)}), bf16[16,32,2048]{2,1,0:T(8,128)(2,1)}, u32[]{:S(2)}, u32[]{:S(2)}) async-start(bf16[16,32,2048]{2,1,0:T(8,128)(2,1)} %bitcast.14), calls=%async_computation.1 | async-start | bytes 4194304 | tf_op jit(solution)/shard_map/all_to_all | solution.py:644
  186.8 1.2 copy-start.12
  188.0 1.2 copy-start.10
  189.3 1.5 copy-start.11
  190.8 1.0 copy-start.13
  196.3 36.6 %copy-start.6 = (bf16[1024,896]{1,0:T(8,128)(2,1)S(1)}, bf16[1024,896]{1,0:T(8,128)(2,1)}, u32[]{:S(2)}) copy-start(bf16[1024,896]{1,0:T(8,128)(2,1)} %constant.148.clone.pack) | copy-start | bytes 5505028
  242.9 1.3 copy-start.2
  244.2 59.6 %copy-start = (bf16[1024,896]{1,0:T(8,128)(2,1)S(1)}, bf16[1024,896]{1,0:T(8,128)(2,1)}, u32[]{:S(2)}) copy-start(bf16[1024,896]{1,0:T(8,128)(2,1)} %copy.45.x.x_ref) | copy-start | bytes 5505028
  303.8 1.5 copy-start.7
  314.3 1.3 copy-start.3
  (5 other events, 4.5 us)

commit v3 on v2

--- a/solution.py
+++ b/solution.py
@@ -307,26 +307,36 @@
 
 
 def front_kernel(
-    x, w, wo, tok, wall, woall, via, y_send, y_recv, c_send, c_recv, w_send, w_recv, o_send, o_recv, l_sem
+    x, w, tok, wall, via, y_send, y_recv, c_send, c_recv, w_send, w_recv, z_send, z_recv, l_sem
 ):
     row, partner, col, across, core, sibling = places()
-    greet([{"row": partner}] + [{"col": lax.rem(col + k, 4)} for k in (1, 2, 3)])
-    size = tok.shape[1] // 2
+    layer = lax.axis_index("req")
+    layers = [lax.rem(layer + k, 4) for k in (1, 2, 3)]
+    greet(
+        [{"row": partner}]
+        + [{"col": lax.rem(col + k, 4)} for k in (1, 2, 3)]
+        + [{"req": other} for other in layers]
+    )
+    parts = c_recv.shape[1]
+    chunks = 2 * parts
+    size = tok.shape[1] // parts
+    quarter = w.shape[0] // 4
 
     def to_row(j):
         rows = pl.ds(j * size, size)
         return remote(x.at[rows], via.at[rows], y_send.at[j], y_recv.at[j], row=partner)
 
     def holder_of(source, j):
-        return 2 * (row if source == 0 else partner) + j // 2
+        return 2 * (row if source == 0 else partner) + j // parts
 
     def ends(source, j):
         src = (x if source == 0 else via).at[pl.ds(j * size, size)]
-        return src, tok.at[col, pl.ds((j % 2) * size, size)], c_recv.at[col, j % 2]
+        part = j % parts
+        return src, tok.at[col, pl.ds(part * size, size)], c_recv.at[col, part]
 
     def to_holder(source, j):
         src, dst, arrival = ends(source, j)
-        return remote(src, dst, c_send.at[source * 4 + j], arrival, col=holder_of(source, j))
+        return remote(src, dst, c_send.at[source * chunks + j], arrival, col=holder_of(source, j))
 
     def start_holder(source, j):
         @pl.when(holder_of(source, j) != col)
@@ -337,35 +347,46 @@
         def _():
             pltpu.make_async_copy(*ends(source, j)).start()
 
-    for j in range(4):
+    def rows_of(at):
+        return pl.ds(pl.multiple_of(at * quarter, 16), quarter)
+
+    def to_layer(k):
+        part = wall.at[across, rows_of(layer)]
+        return remote(part, part, z_send.at[k], z_recv.at[k], req=layers[k])
+
+    mine = rows_of(layer)
+    w_across = remote(w.at[mine], wall.at[col, mine], w_send.at[0], w_recv.at[0], col=across)
+    w_side = remote(w, wall.at[col], w_send.at[1], w_recv.at[1], col=sibling)
+    w_on = remote(wall.at[across], wall.at[across], w_send.at[2], w_recv.at[2], col=sibling)
+    w_here = pltpu.make_async_copy(w, wall.at[col], l_sem)
+    w_across.start()
+    for j in range(chunks):
         to_row(j).start()
-    w_across = remote(w, wall.at[col], w_send.at[0], w_recv.at[0], col=across)
-    w_side = remote(w, wall.at[col], w_send.at[1], w_recv.at[1], col=sibling)
-    w_here = pltpu.make_async_copy(w, wall.at[col], l_sem.at[0])
-    o_there = remote(wo, woall.at[row], o_send, o_recv, row=partner)
-    o_here = pltpu.make_async_copy(wo, woall.at[row], l_sem.at[1])
-    for j in range(4):
+    for j in range(chunks):
         start_holder(0, j)
-    w_across.start()
     w_side.start()
     w_here.start()
-    o_here.start()
-    for j in range(4):
+    for j in range(chunks):
+        if j == 2:
+            got = wall.at[across, mine]
+            remote(got, got, w_send.at[0], w_recv.at[0], col=across).wait_recv()
+            for k in range(3):
+                to_layer(k).start()
         to_row(j).wait_recv()
         start_holder(1, j)
-    o_there.start()
-    w_across.wait_recv()
-    w_on = remote(wall.at[across], wall.at[across], w_send.at[2], w_recv.at[2], col=sibling)
+    for k in range(3):
+        got = wall.at[across, rows_of(lax.rem(layer + 3 - k, 4))]
+        remote(got, got, z_send.at[k], z_recv.at[k], req=layers[k]).wait_recv()
     w_on.start()
     for source in range(2):
-        for j in range(4):
+        for j in range(chunks):
 
             @pl.when(holder_of(source, j) != col)
             def _():
                 to_holder(source, j).wait_send()
 
     for k in range(4):
-        for part in range(2):
+        for part in range(parts):
             rows = pl.ds(part * size, size)
 
             @pl.when(col != k)
@@ -378,39 +399,38 @@
             def _():
                 pltpu.make_async_copy(tok.at[k, rows], tok.at[k, rows], c_recv.at[k, part]).wait()
 
-    for j in range(4):
+    for j in range(chunks):
         to_row(j).wait_send()
+    for k in range(3):
+        to_layer(k).wait_send()
     w_across.wait_send()
     w_side.wait()
     w_on.wait()
     w_here.wait()
-    o_there.wait()
-    o_here.wait()
-
-
-def front(x, w, wo, conts):
+
+
+def front(x, w, conts):
     dma = pltpu.SemaphoreType.DMA
     return pl.pallas_call(
         front_kernel,
-        in_specs=[pl.BlockSpec(memory_space=pl.ANY)] * 3,
-        out_specs=[pl.BlockSpec(memory_space=pl.ANY)] * 4,
+        in_specs=[pl.BlockSpec(memory_space=pl.ANY)] * 2,
+        out_specs=[pl.BlockSpec(memory_space=pl.ANY)] * 3,
         out_shape=[
             jax.ShapeDtypeStruct((4, conts, x.shape[1]), BF16),
             jax.ShapeDtypeStruct((4,) + w.shape, BF16),
-            jax.ShapeDtypeStruct((2,) + wo.shape, BF16),
             jax.ShapeDtypeStruct(x.shape, BF16),
         ],
         scratch_shapes=[
-            dma((4,)), dma((4,)), dma((8,)), dma((4, 2)), dma((3,)), dma((3,)), dma, dma, dma((2,)),
+            dma((8,)), dma((8,)), dma((16,)), dma((4, 4)), dma((3,)), dma((3,)), dma((3,)), dma((3,)), dma,
         ],
         compiler_params=pltpu.CompilerParams(collective_id=0, has_side_effects=True),
-    )(x, w, wo)
+    )(x, w)
 
 
 def back_kernel(h, hall, via, sx, rx, sy, ry, ss, rs, sf, rf, sl):
     row, partner, col, across, core, sibling = places()
     greet([{"row": partner}, {"col": across}, {"col": sibling}])
-    pieces = 4
+    pieces = 8
     size = h.shape[0] // pieces
     stays = col // 2 == row
 
@@ -424,25 +444,25 @@
         return remote(at(h, j), at(via, j), sx.at[j], rx.at[j], col=across)
 
     def x_final(j):
-        return remote(at(h, j), slot(core, row, j), sx.at[j], rx.at[j], col=across)
+        return remote(at(h, j), slot(core, 0, j), sx.at[j], rx.at[j], col=across)
 
     def y_own(j):
-        return remote(at(h, j), slot(core, row, j), sy.at[j], ry.at[j], row=partner)
+        return remote(at(h, j), slot(core, 1, j), sy.at[j], ry.at[j], row=partner)
 
     def y_via(j):
-        return remote(at(via, j), slot(core, row, j), sy.at[j], ry.at[j], row=partner)
+        return remote(at(via, j), slot(core, 1, j), sy.at[j], ry.at[j], row=partner)
 
     def side_own(j):
-        return remote(at(h, j), slot(core, row, j), ss.at[j], rs.at[j], col=sibling)
+        return remote(at(h, j), slot(core, 0, j), ss.at[j], rs.at[j], col=sibling)
 
     def side_got(j):
-        return remote(slot(core, row, j), slot(core, row, j), ss.at[j], rs.at[j], col=sibling)
+        return remote(slot(core, 0, j), slot(core, 0, j), ss.at[j], rs.at[j], col=sibling)
 
     def side_far(j):
-        return remote(slot(core, partner, j), slot(core, partner, j), sf.at[j], rf.at[j], col=sibling)
+        return remote(slot(core, 1, j), slot(core, 1, j), sf.at[j], rf.at[j], col=sibling)
 
     def keep(j):
-        return pltpu.make_async_copy(at(h, j), slot(core, row, j), sl.at[j])
+        return pltpu.make_async_copy(at(h, j), slot(core, 0, j), sl.at[j])
 
     for j in range(pieces):
 
@@ -466,15 +486,15 @@
 
         @pl.when(jnp.logical_not(stays))
         def _():
-            remote(slot(core, row, j), slot(core, row, j), sx.at[j], rx.at[j], col=across).wait_recv()
+            remote(slot(core, 0, j), slot(core, 0, j), sx.at[j], rx.at[j], col=across).wait_recv()
             side_got(j).start()
 
     for j in range(pieces):
-        remote(slot(core, partner, j), slot(core, partner, j), sy.at[j], ry.at[j], row=partner).wait_recv()
+        remote(slot(core, 1, j), slot(core, 1, j), sy.at[j], ry.at[j], row=partner).wait_recv()
         side_far(j).start()
     for j in range(pieces):
-        near = slot(1 - core, row, j)
-        far = slot(1 - core, partner, j)
+        near = slot(1 - core, 0, j)
+        far = slot(1 - core, 1, j)
         remote(near, near, ss.at[j], rs.at[j], col=sibling).wait_recv()
         remote(far, far, sf.at[j], rf.at[j], col=sibling).wait_recv()
         side_far(j).wait_send()
@@ -494,7 +514,7 @@
 
 
 def back(h):
-    dma = pltpu.SemaphoreType.DMA((4,))
+    dma = pltpu.SemaphoreType.DMA((8,))
     return pl.pallas_call(
         back_kernel,
         in_specs=[pl.BlockSpec(memory_space=pl.ANY)],
@@ -586,18 +606,16 @@
     capacity = (slots // 2 + holders - 2) // (holders - 1)
     me = lax.axis_index(axes)
 
-    pair = jnp.stack([slot_prompt // slots, slot_prompt % slots]).astype(BF16)
-    pair = jnp.zeros((16, LANES), BF16).at[:2, :slots].set(pair)
-    pairs = lax.all_gather(pair, axes, axis=0, tiled=True).reshape(holders, 16, LANES)[:, :2, :slots]
-    pairs = pairs.astype(jnp.int32)
-    every = (pairs[:, 0] * slots + pairs[:, 1]).reshape(-1)
+    copies = jnp.broadcast_to(slot_prompt[None, None], (holders, 1, slots))
+    every = lax.all_to_all(copies, axes, split_axis=0, concat_axis=0, tiled=True).reshape(-1)
     flat = tokens.reshape(tokens.shape[0], 2 * depth)
     value_weight = jnp.moveaxis(w_value.reshape(heads, depth, HEAD_DIM), 0, 1).reshape(depth, hd)
     stacked = jnp.concatenate([w_query, w_key, value_weight], axis=1)
-    direct = lax.axis_size("row") == 2 and lax.axis_size("col") == 4
+    direct = lax.axis_size("row") == 2 and lax.axis_size("col") == lax.axis_size("req") == 4
     if direct:
-        tok, w_all, wo_all, _ = front(flat, stacked, w_out, conts)
-        projected = project(tok, w_all)
+        tok, w_all, _ = front(flat, stacked, conts)
+        projected, wo_own = lax.optimization_barrier((project(tok, w_all), w_out))
+        wo_all = jnp.stack([wo_own, lax.ppermute(wo_own, "row", [(0, 1), (1, 0)])])
     else:
         gathered = lax.all_gather(flat, "row", axis=0, tiled=True)
         partial_sums = [

time: 321 us -> 288 us (0.90)
  Pallas kernels: 239 us -> 213 us
  blocking collectives: 19.5 us -> 0 us
  starting transfers between devices: 12.9 us -> 19 us
  waiting for transfers between devices: 10.4 us -> 15.1 us
    pallas_call x1, Pallas kernels: 89.5 us -> 62.8 us  [front(): pl.pallas_call(front_kernel, in_specs=[pl.BlockSpec(memory_space=pl.ANY)]...]
    all_gather x1 -> x0, blocking collectives: 19.5 us -> none  [body(): lax.all_gather(pair, axes, axis=0, tiled=True).reshape(holders, 16, LANES)]
    all_to_all x1, waiting for transfers between devices: 0.01 us -> 8.49 us  [body(): lax.all_to_all(outgoing.reshape(holders, capacity * per, 2 * hf), axes, s...]
    all_to_all x0 -> x1, starting transfers between devices: none -> 6.58 us  [body(): lax.all_to_all(copies, axes, split_axis=0, concat_axis=0, tiled=True)]
    unnamed x56 -> x55, local copies, waits for them, and re-layouts: 16.8 us -> 11.1 us
    all_to_all x1, waiting for transfers between devices: 10.4 us -> 6.62 us  [body(): lax.all_to_all(replies.reshape(holders, capacity * per, -1), axes, split_...]
  transfers between devices with their start and end apart: 2 -> 4, of which waited for: 1 -> 2; matrix products, arithmetic and copies ran while one was open for 0% -> 6% of each run, Pallas kernels for 14% -> 41%
where the time goes in v3:
time: 288 us; the launch traced here: 287 us
  Pallas kernels  213 us (74%)
  local copies, waits for them, and re-layouts  27.8 us (10%)
  starting transfers between devices  19 us (7%)
  waiting for transfers between devices  15.1 us (5%)
  other arithmetic  6.83 us (2%)
  matrix products  4.36 us (2%)
    pallas_call x1, Pallas kernels, front(): pl.pallas_call(front_kernel, in_specs=[pl.BlockSpec(memory_space=pl.ANY)]...  62.8 us
    pallas_call x1, Pallas kernels, back(): pl.pallas_call(back_kernel, in_specs=[pl.BlockSpec(memory_space=pl.ANY)],...  59.9 us
    pallas_call x1, Pallas kernels, tail_terms(): pl.pallas_call(functools.partial(tail_kernel, heads, tail), grid=(conts /...  26.1 us
    pallas_call x1, Pallas kernels, turn_states(): pl.pallas_call(state_kernel, grid=(heads,), in_specs=[pl.BlockSpec((width...  19.1 us
    pallas_call x1, Pallas kernels, prompt_terms(): pl.pallas_call(prompt_kernel, grid=(heads,), in_specs=[pl.BlockSpec(slot_...  17.9 us
    unnamed x55, local copies, waits for them, and re-layouts  11.1 us
    pallas_call x1, Pallas kernels, combine(): pl.pallas_call(functools.partial(combine_kernel, heads), grid=(conts // b...  9.91 us
    pallas_call x1, Pallas kernels, output(): pl.pallas_call(output_kernel, grid=(2, steps), in_specs=[pl.BlockSpec((1,...  9 us
  transfers between devices with their start and end apart: 4, of which 2 were waited for; matrix products, arithmetic and copies ran while one was open for 6% of the time, Pallas kernels for 41%

profile of v3, /device:TPU:9, one launch (start us, length us, event | category | flops | bytes accessed | tf_op | source)
XLA Modules:
  0.0 286.9 jit_solution(13436843499159584115)
XLA Ops:
  0.0 1.3 broadcast_in_dim.43
  1.3 6.6 %all-to-all-start = ((s32[16,1,32]{2,1,0:T(1,128)}), s32[16,1,32]{2,1,0:T(1,128)S(1)}, u32[]{:S(2)}, u32[]{:S(2)}) async-start(s32[16,1,32]{2,1,0:T(1,128)} %broadcast_in_dim.43), calls=%async_computation | async-start | bytes 16384 | tf_op jit(solution)/shard_map/all_to_all | solution.py:610
  8.6 3.8 %copy.77.x.x_ref = bf16[1024,896]{1,0:T(8,128)(2,1)} copy(bf16[1024,896]{0,1:T(8,128)(2,1)} %bitcast.27) | data formatting | bytes 3670016 | tf_op jit(solution)/shard_map/reshape | solution.py:611
  12.4 1.3 reshape.296
  16.2 62.8 %shard_map.226 = (bf16[4,512,896]{2,1,0:T(8,128)(2,1)}, bf16[4,448,1152]{2,1,0:T(8,128)(2,1)}, bf16[1024,896]{1,0:T(8,128)(2,1)}) custom-call(bf16[1024,896]{1,0:T(8,128)(2,1)} %copy.77.x.x_ref, bf16[448,1152]{1,0:T(8,128)(2,1)} %pad_maximum_fusion.1.w), custom_call_target="tpu_custom_call" | custom-call | tf_op jit(solution)/shard_map/pallas_call | solution.py:414
  79.0 2.0 copy-done.5
  81.0 8.7 %shard_map.227.q_ref = bf16[512,2304]{1,0:T(8,128)(2,1)S(1)} custom-call(bf16[4,512,896]{2,1,0:T(8,128)(2,1)S(1)} %copy-done.5, bf16[4,448,1152]{2,1,0:T(8,128)(2,1)} %get-tuple-element.11.w_ref), custom_call_target="tpu_custom_call" | custom-call | tf_op jit(solution)/shard_map/pallas_call | solution.py:543
  90.0 19.1 %shard_map.229.states_ref = bf16[8,32,128,384]{3,2,1,0:T(8,128)(2,1)} custom-call(bf16[256,256]{1,0:T(8,128)(2,1)S(1)} %copy-done.18, bf16[1,273,28672]{2,1,0:T(8,128)(2,1)} %state_ref.1, bf16[8,32,273]{2,1,0:T(8,128)(2,1)S(1)} %bitcast.22), custom_call_target="tpu_custom_call" | custom-call | flops 20000000000 | bytes 45000000 | tf_op jit(solution)/shard_map/pallas_call | solution.py:64
  112.6 5.5 %all-to-all-start.1 = ((bf16[16,32,256]{2,1,0:T(8,128)(2,1)}), bf16[16,32,256]{2,1,0:T(8,128)(2,1)S(1)}, u32[]{:S(2)}, u32[]{:S(2)}) async-start(bf16[16,32,256]{2,1,0:T(8,128)(2,1)} %bitcast.8), calls=%async_computation.1 | async-start | bytes 524288 | tf_op jit(solution)/shard_map/all_to_all | solution.py:654
  118.3 8.5 %all-to-all-done.1 = bf16[16,32,256]{2,1,0:T(8,128)(2,1)S(1)} async-done(((bf16[16,32,256]{2,1,0:T(8,128)(2,1)}), bf16[16,32,256]{2,1,0:T(8,128)(2,1)S(1)}, u32[]{:S(2)}, u32[]{:S(2)}) %all-to-all-start.1) | async-done | bytes 262176 | tf_op jit(solution)/shard_map/all_to_all | solution.py:654
  127.5 17.9 %shard_map.230.kept_ref = bf16[512,2048]{1,0:T(8,128)(2,1)S(1)} custom-call(bf16[512,256]{1,0:T(8,128)(2,1)S(1)} %fusion.q_ref, bf16[8,128,768]{2,1,0:T(8,128)(2,1)S(1)} %copy-done.8, f32[8,384]{1,0:T(8,128)S(1)} %copy-done.9, bf16[8,32,128,384]{3,2,1,0:T(8,128)(2,1)} %shard_map.229.states_ref), custom_call_target="tpu_custom_call" | custom-call | tf_op jit(solution)/shard_map/pallas_call | solution.py:132
  145.4 2.7 convolution_convert_fusion
  148.1 5.9 %all-to-all-start.2 = ((bf16[16,32,2048]{2,1,0:T(8,128)(2,1)}), bf16[16,32,2048]{2,1,0:T(8,128)(2,1)}, u32[]{:S(2)}, u32[]{:S(2)}) async-start(bf16[16,32,2048]{2,1,0:T(8,128)(2,1)} %bitcast.26), calls=%async_computation.2 | async-start | bytes 4194304 | tf_op jit(solution)/shard_map/all_to_all | solution.py:662
  160.1 26.1 %shard_map.228.acc_ref = f32[512,2048]{1,0:T(8,128)} custom-call(bf16[512,2304]{1,0:T(8,128)(2,1)} %copy-done.6, bf16[512,1024]{1,0:T(8,128)(2,1)S(1)} %copy-done.10, bf16[512,7168]{1,0:T(8,128)(2,1)} %tv_ref.1, s32[512,1]{1,0:T(8,128)S(1)} %copy.78.len_ref, bf16[128,1024]{1,0:T(8,128)(2,1)S(1)} %copy-done.14, bf16[1024,64]{1,0:T(8,128)(2,1)S(1)} %copy-done.15, ...), custom_call_target="tpu_custom_call" | custom-call | flops 20000000000 | bytes 25000000 | tf_op jit(solution)/shard_map/pallas_call | solution.py:222
  186.2 1.5 copy.87
  188.4 2.3 copy.88
  190.8 2.8 pad_maximum_fusion.w_ref
  193.5 6.6 %all-to-all-done.2 = bf16[16,32,2048]{2,1,0:T(8,128)(2,1)} async-done(((bf16[16,32,2048]{2,1,0:T(8,128)(2,1)}), bf16[16,32,2048]{2,1,0:T(8,128)(2,1)}, u32[]{:S(2)}, u32[]{:S(2)}) %all-to-all-start.2) | async-done | bytes 2097184 | tf_op jit(solution)/shard_map/all_to_all | solution.py:662
  200.1 9.9 %shard_map.231.h = bf16[512,1792]{1,0:T(8,128)(2,1)S(1)} custom-call(f32[512,2048]{1,0:T(8,128)} %shard_map.228.acc_ref, s32[512,1]{1,0:T(8,128)S(1)} %get-tuple-element.22.sent_at, s32[512,1]{1,0:T(8,128)S(1)} %get-tuple-element.21.kept_at, bf16[512,2048]{1,0:T(8,128)(2,1)} %bitcast.12.got_ref, bf16[512,2048]{1,0:T(8,128)(2,1)} %copy-done.1, ...), custom_call_target="tpu_custom_call" | custom-call | tf_op jit(solution)/shard_map/pallas_call | solution.py:273
  210.1 1.3 copy-done.3
  211.4 59.9 %shard_map.232 = (bf16[2,2,512,1792]{3,2,1,0:T(8,128)(2,1)}, bf16[512,1792]{1,0:T(8,128)(2,1)}) custom-call(bf16[512,1792]{1,0:T(8,128)(2,1)} %copy-done.3), custom_call_target="tpu_custom_call" | custom-call | tf_op jit(solution)/shard_map/pallas_call | solution.py:518
  271.4 1.5 copy-done.2
  272.9 9.0 %shard_map.233 = bf16[1024,896]{1,0:T(8,128)(2,1)S(1)} custom-call(bf16[2,2,512,1792]{3,2,1,0:T(8,128)(2,1)} %get-tuple-element.13.h_ref, bf16[2,896,448]{2,1,0:T(8,128)(2,1)S(1)} %copy-done.2, bf16[1024,896]{1,0:T(8,128)(2,1)S(1)} %copy-done), custom_call_target="tpu_custom_call" | custom-call | tf_op jit(solution)/shard_map/pallas_call | solution.py:569
  283.1 3.8 %copy.90 = bf16[1024,896]{0,1:T(8,128)(2,1)} copy(bf16[1024,896]{1,0:T(8,128)(2,1)} %copy-done.4) | data formatting | bytes 3670016 | tf_op jit(solution)/shard_map/pallas_call | solution.py:569
  (84 shorter events, 15.7 us)
Async XLA Ops:
  0.0 12.4 %copy-start.20 = (bf16[8,50176]{1,0:T(8,128)(2,1)S(1)}, bf16[8,50176]{1,0:T(8,128)(2,1)}, u32[]{:S(2)}) copy-start(bf16[8,50176]{1,0:T(8,128)(2,1)} %param.27) | copy-start | bytes 2408452
  1.3 107.8 %all-to-all-start = ((s32[16,1,32]{2,1,0:T(1,128)}), s32[16,1,32]{2,1,0:T(1,128)S(1)}, u32[]{:S(2)}, u32[]{:S(2)}) async-start(s32[16,1,32]{2,1,0:T(1,128)} %broadcast_in_dim.43), calls=%async_computation | async-start | bytes 16384 | tf_op jit(solution)/shard_map/all_to_all | solution.py:610
  13.7 1.4 copy-start.22
  13.7 1.4 copy-start.23
  79.0 2.0 copy-start.5
  81.0 8.9 %copy-start.21 = (bf16[32,273,8]{1,2,0:T(8,128)(2,1)S(1)}, bf16[32,273,8]{1,2,0:T(8,128)(2,1)}, u32[]{:S(2)}) copy-start(bf16[32,273,8]{1,2,0:T(8,128)(2,1)} %param.30) | copy-start | bytes 419332
  81.0 8.9 %copy-start.24 = (s32[512]{0:T(512)S(1)}, s32[512]{0:T(512)}, u32[]{:S(2)}) copy-start(s32[512]{0:T(512)} %param.32) | copy-start | bytes 6148
  81.0 9.0 %copy-start.18 = (bf16[256,256]{1,0:T(8,128)(2,1)S(1)}, bf16[256,256]{1,0:T(8,128)(2,1)}, u32[]{:S(2)}) copy-start(bf16[256,256]{1,0:T(8,128)(2,1)} %constant.99.clone.perm_ref) | copy-start | bytes 393220
  89.7 19.4 %copy-start.6 = (bf16[512,2304]{1,0:T(8,128)(2,1)}, bf16[512,2304]{1,0:T(8,128)(2,1)S(1)}, u32[]{:S(2)}) copy-start(bf16[512,2304]{1,0:T(8,128)(2,1)S(1)} %shard_map.227.q_ref) | copy-start | bytes 7077892
  90.0 28.1 %copy-start.26 = (s32[32]{0:T(128)S(1)}, s32[32]{0:T(128)}, u32[]{:S(2)}) copy-start(s32[32]{0:T(128)} %param.31) | copy-start | bytes 388
  109.1 18.4 %copy-start.9 = (f32[8,384]{1,0:T(8,128)S(1)}, f32[8,384]{1,0:T(8,128)}, u32[]{:S(2)}) copy-start(f32[8,384]{1,0:T(8,128)} %constant.109.clone.shift_ref) | copy-start | bytes 36868
  109.1 18.4 %copy-start.8 = (bf16[8,128,768]{2,1,0:T(8,128)(2,1)S(1)}, bf16[8,128,768]{2,1,0:T(8,128)(2,1)}, u32[]{:S(2)}) copy-start(bf16[8,128,768]{2,1,0:T(8,128)(2,1)} %constant.108.clone.pick_ref) | copy-start | bytes 4718596
  112.6 14.2 %all-to-all-start.1 = ((bf16[16,32,256]{2,1,0:T(8,128)(2,1)}), bf16[16,32,256]{2,1,0:T(8,128)(2,1)S(1)}, u32[]{:S(2)}, u32[]{:S(2)}) async-start(bf16[16,32,256]{2,1,0:T(8,128)(2,1)} %bitcast.8), calls=%async_computation.1 | async-start | bytes 524288 | tf_op jit(solution)/shard_map/all_to_all | solution.py:654
  145.4 2.7 copy-start.1
  148.1 6.9 %copy-start.25 = (s32[512]{0:T(512)S(1)}, s32[512]{0:T(512)}, u32[]{:S(2)}) copy-start(s32[512]{0:T(512)} %param.35) | copy-start | bytes 6148
  148.1 7.1 %copy-start.10 = (bf16[512,1024]{1,0:T(8,128)(2,1)S(1)}, bf16[512,1024]{1,0:T(8,128)(2,1)}, u32[]{:S(2)}) copy-start(bf16[512,1024]{1,0:T(8,128)(2,1)} %tk_ref.1) | copy-start | bytes 3145732
  148.1 7.1 %copy-start.11 = (bf16[896,1024]{1,0:T(8,128)(2,1)S(1)}, bf16[896,1024]{1,0:T(8,128)(2,1)}, u32[]{:S(2)}) copy-start(bf16[896,1024]{1,0:T(8,128)(2,1)} %constant.107.clone.pad) | copy-start | bytes 5505028
  148.1 7.1 %copy-start.14 = (bf16[128,1024]{1,0:T(8,128)(2,1)S(1)}, bf16[128,1024]{1,0:T(8,128)(2,1)}, u32[]{:S(2)}) copy-start(bf16[128,1024]{1,0:T(8,128)(2,1)} %constant.100.clone.eq) | copy-start | bytes 786436
  148.1 7.1 %copy-start.17 = (bf16[64,1024]{1,0:T(8,128)(2,1)S(1)}, bf16[64,1024]{1,0:T(8,128)(2,1)}, u32[]{:S(2)}) copy-start(bf16[64,1024]{1,0:T(8,128)(2,1)} %constant.104.clone.dw) | copy-start | bytes 393220
  148.1 52.1 %all-to-all-start.2 = ((bf16[16,32,2048]{2,1,0:T(8,128)(2,1)}), bf16[16,32,2048]{2,1,0:T(8,128)(2,1)}, u32[]{:S(2)}, u32[]{:S(2)}) async-start(bf16[16,32,2048]{2,1,0:T(8,128)(2,1)} %bitcast.26), calls=%async_computation.2 | async-start | bytes 4194304 | tf_op jit(solution)/shard_map/all_to_all | solution.py:662
  154.0 34.4 %collective-permute-start = (bf16[896,448]{0,1:T(8,128)(2,1)}, bf16[896,448]{0,1:T(8,128)(2,1)}, u32[]{:S(2)}, u32[]{:S(2)}) collective-permute-start(bf16[896,448]{0,1:T(8,128)(2,1)} %param.28), channel_id=1, source_target_pairs={{0,4},{4,0},{1,5},{5,1},{2,6},{6,2},{3,7},{7,3},{8,12},{12,8},{9,1... | collective-permute-start | bytes 2408456 | tf_op jit(solution)/shard_map/ppermute | solution.py:618
  190.8 9.4 %copy-start.7 = (bf16[1024,896]{1,0:T(8,128)(2,1)S(1)}, bf16[1024,896]{1,0:T(8,128)(2,1)}, u32[]{:S(2)}) copy-start(bf16[1024,896]{1,0:T(8,128)(2,1)} %constant.110.clone.pack) | copy-start | bytes 5505028
  211.4 60.0 %copy-start = (bf16[1024,896]{1,0:T(8,128)(2,1)S(1)}, bf16[1024,896]{1,0:T(8,128)(2,1)}, u32[]{:S(2)}) copy-start(bf16[1024,896]{1,0:T(8,128)(2,1)} %copy.77.x.x_ref) | copy-start | bytes 5505028
  271.4 1.5 copy-start.2
  (7 other events, 7.5 us)

commit v4 on v3

--- a/solution.py
+++ b/solution.py
@@ -254,14 +254,18 @@
         out_ref[:, t * hd : (t + 1) * hd] = dot(wide, pack[...]).astype(BF16)
 
 
+def pack_table(heads):
+    pack = np.zeros((heads * LANES, heads * HEAD_DIM), np.float32)
+    entries = np.arange(HEAD_DIM)
+    for h in range(heads):
+        pack[h * LANES + entries, h * HEAD_DIM + entries] = 1
+    return jnp.asarray(pack, BF16)
+
+
 def combine(acc, sent_at, kept_at, got, kept, heads):
     conts = acc.shape[0]
     block = min(conts, 128)
     hd = heads * HEAD_DIM
-    pack = np.zeros((heads * LANES, hd), np.float32)
-    entries = np.arange(HEAD_DIM)
-    for h in range(heads):
-        pack[h * LANES + entries, h * HEAD_DIM + entries] = 1
 
     def rows(array):
         return pl.BlockSpec((block, array.shape[1]), lambda i: (i, 0))
@@ -269,7 +273,7 @@
     def whole(array):
         return pl.BlockSpec(array.shape, lambda i: (0, 0))
 
-    pack = jnp.asarray(pack, BF16)
+    pack = pack_table(heads)
     return pl.pallas_call(
         functools.partial(combine_kernel, heads),
         grid=(conts // block,),
@@ -427,7 +431,9 @@
     )(x, w)
 
 
-def back_kernel(h, hall, via, sx, rx, sy, ry, ss, rs, sf, rf, sl):
+def back_kernel(
+    heads, acc, sent_at, kept_at, got, kept, pack, w, x, out, h, hall, via, sx, rx, sy, ry, ss, rs, sf, rf, sl
+):
     row, partner, col, across, core, sibling = places()
     greet([{"row": partner}, {"col": across}, {"col": sibling}])
     pieces = 8
@@ -435,10 +441,10 @@
     stays = col // 2 == row
 
     def at(ref, j):
-        return ref.at[pl.ds(j * size, size)]
+        return ref.at[pl.ds(pl.multiple_of(j * size, size), size)]
 
     def slot(b, half, j):
-        return hall.at[b, half, pl.ds(j * size, size)]
+        return hall.at[b, half, pl.ds(pl.multiple_of(j * size, size), size)]
 
     def x_via(j):
         return remote(at(h, j), at(via, j), sx.at[j], rx.at[j], col=across)
@@ -464,19 +470,30 @@
     def keep(j):
         return pltpu.make_async_copy(at(h, j), slot(core, 0, j), sl.at[j])
 
-    for j in range(pieces):
-
-        @pl.when(stays)
-        def _():
-            x_final(j).start()
-            side_own(j).start()
-            keep(j).start()
-
-        @pl.when(jnp.logical_not(stays))
-        def _():
-            x_via(j).start()
-            y_own(j).start()
-
+    block = 2 * size
+    count = pieces // 2
+
+    def sums(i, carry):
+        rows = pl.ds(pl.multiple_of(i * block, block), block)
+        parts = [acc.at[rows], sent_at.at[rows], kept_at.at[rows]]
+        combine_kernel(heads, *parts, got, kept, pack, h.at[rows])
+        for extra in range(2):
+            j = 2 * i + extra
+
+            @pl.when(stays)
+            def _():
+                x_final(j).start()
+                side_own(j).start()
+                keep(j).start()
+
+            @pl.when(jnp.logical_not(stays))
+            def _():
+                x_via(j).start()
+                y_own(j).start()
+
+        return carry
+
+    lax.fori_loop(0, count, sums, 0)
     for j in range(pieces):
 
         @pl.when(stays)
@@ -489,14 +506,37 @@
             remote(slot(core, 0, j), slot(core, 0, j), sx.at[j], rx.at[j], col=across).wait_recv()
             side_got(j).start()
 
+    hd, depth = w.shape[1:]
+
+    def products(i):
+        for j in (2 * i, 2 * i + 1):
+            near, far = slot(1 - core, 0, j), slot(1 - core, 1, j)
+            remote(near, near, ss.at[j], rs.at[j], col=sibling).wait_recv()
+            remote(far, far, sf.at[j], rf.at[j], col=sibling).wait_recv()
+
+            @pl.when(stays)
+            def _():
+                keep(j).wait()
+
+        rows = pl.ds(i * block, block)
+        for b in range(2):
+            place = pl.ds(b * h.shape[0] + i * block, block)
+            for t in range(2):
+                total = x[place, t * depth : (t + 1) * depth].astype(F32)
+                for half in range(2):
+                    part = dot(hall[b, half, rows, t * hd : (t + 1) * hd], w[half])
+                    total = total + part.astype(BF16).astype(F32)
+                out[place, t * depth : (t + 1) * depth] = total.astype(BF16)
+
+    for i in range(count):
+        for j in (2 * i, 2 * i + 1):
+            far = slot(core, 1, j)
+            remote(far, far, sy.at[j], ry.at[j], row=partner).wait_recv()
+            side_far(j).start()
+        if i > 0:
+            products(i - 1)
+    products(count - 1)
     for j in range(pieces):
-        remote(slot(core, 1, j), slot(core, 1, j), sy.at[j], ry.at[j], row=partner).wait_recv()
-        side_far(j).start()
-    for j in range(pieces):
-        near = slot(1 - core, 0, j)
-        far = slot(1 - core, 1, j)
-        remote(near, near, ss.at[j], rs.at[j], col=sibling).wait_recv()
-        remote(far, far, sf.at[j], rf.at[j], col=sibling).wait_recv()
         side_far(j).wait_send()
 
         @pl.when(stays)
@@ -504,7 +544,6 @@
             x_final(j).wait_send()
             y_via(j).wait_send()
             side_own(j).wait_send()
-            keep(j).wait()
 
         @pl.when(jnp.logical_not(stays))
         def _():
@@ -513,19 +552,21 @@
             side_got(j).wait_send()
 
 
-def back(h):
+def back(acc, sent_at, kept_at, got, kept, w, flat, heads):
     dma = pltpu.SemaphoreType.DMA((8,))
+    conts, hd = acc.shape[0], heads * HEAD_DIM
+    wide = (conts, 2 * hd)
     return pl.pallas_call(
-        back_kernel,
-        in_specs=[pl.BlockSpec(memory_space=pl.ANY)],
-        out_specs=[pl.BlockSpec(memory_space=pl.ANY)] * 2,
-        out_shape=[
-            jax.ShapeDtypeStruct((2, 2) + h.shape, BF16),
-            jax.ShapeDtypeStruct(h.shape, BF16),
-        ],
-        scratch_shapes=[dma] * 9,
-        compiler_params=pltpu.CompilerParams(collective_id=1, has_side_effects=True),
-    )(h)[0]
+        functools.partial(back_kernel, heads),
+        in_specs=[pl.BlockSpec(memory_space=pltpu.VMEM)] * 8,
+        out_specs=pl.BlockSpec(memory_space=pltpu.VMEM),
+        out_shape=jax.ShapeDtypeStruct(flat.shape, BF16),
+        scratch_shapes=[pltpu.VMEM(wide, BF16), pltpu.VMEM((2, 2) + wide, BF16), pltpu.VMEM(wide, BF16)]
+        + [dma] * 9,
+        compiler_params=pltpu.CompilerParams(
+            collective_id=1, has_side_effects=True, vmem_limit_bytes=VMEM_LIMIT
+        ),
+    )(acc, sent_at, kept_at, got, kept, pack_table(heads), w, flat)
 
 
 def project_kernel(tok_ref, w_ref, out_ref):
@@ -551,33 +592,6 @@
         out_shape=jax.ShapeDtypeStruct((conts, 2 * total), BF16),
         compiler_params=pltpu.CompilerParams(vmem_limit_bytes=VMEM_LIMIT),
     )(tok, w)
-
-
-def output_kernel(h_ref, w_ref, x_ref, out_ref):
-    hd, depth = w_ref.shape[1:]
-    for t in range(2):
-        acc = x_ref[:, t * depth : (t + 1) * depth].astype(F32)
-        for half in range(2):
-            part = dot(h_ref[0, half, :, t * hd : (t + 1) * hd], w_ref[half])
-            acc = acc + part.astype(BF16).astype(F32)
-        out_ref[:, t * depth : (t + 1) * depth] = acc.astype(BF16)
-
-
-def output(hall, w, flat):
-    block = 128
-    steps = hall.shape[2] // block
-    return pl.pallas_call(
-        output_kernel,
-        grid=(2, steps),
-        in_specs=[
-            pl.BlockSpec((1, 2, block, hall.shape[3]), lambda b, i: (b, 0, i, 0)),
-            pl.BlockSpec(w.shape, lambda b, i: (0, 0, 0)),
-            pl.BlockSpec((block, flat.shape[1]), lambda b, i: (b * steps + i, 0)),
-        ],
-        out_specs=pl.BlockSpec((block, flat.shape[1]), lambda b, i: (b * steps + i, 0)),
-        out_shape=jax.ShapeDtypeStruct(flat.shape, BF16),
-        compiler_params=pltpu.CompilerParams(vmem_limit_bytes=VMEM_LIMIT),
-    )(hall, w, flat)
 
 
 def body(
@@ -624,7 +638,6 @@
         projected = lax.psum_scatter(
             jnp.concatenate(partial_sums, axis=1), "col", scatter_dimension=0, tiled=True
         )
-    states = turn_states(cached_state, jnp.transpose(cached_norm, (2, 0, 1)), heads, slots)
 
     owner = (every // slots).reshape(holders, slots)
     before = jnp.arange(slots)[None, :] < jnp.arange(slots)[:, None]
@@ -651,6 +664,8 @@
     total = 2 * hf + hd
     queries = jnp.concatenate([projected[:, :hf], projected[:, total : total + hf]], axis=1)
     outgoing = dot((sends[:, None] == sent_at[None, :]).astype(BF16), queries).astype(BF16)
+    norm, outgoing = lax.optimization_barrier((jnp.transpose(cached_norm, (2, 0, 1)), outgoing))
+    states = turn_states(cached_state, norm, heads, slots)
     incoming = lax.all_to_all(
         outgoing.reshape(holders, capacity * per, 2 * hf), axes, split_axis=0, concat_axis=0, tiled=True
     ).reshape(-1, 2 * hf)
@@ -662,10 +677,11 @@
     answers = lax.all_to_all(
         replies.reshape(holders, capacity * per, -1), axes, split_axis=0, concat_axis=0, tiled=True
     ).reshape(replies.shape)
-    heads_out = combine(acc, sent_at[:, None], kept_at[:, None], answers, prompt, heads)
-
+    sums = (acc, sent_at[:, None], kept_at[:, None], answers, prompt)
     if direct:
-        return output(back(heads_out), wo_all, flat).reshape(tokens.shape)
+        return back(*sums, wo_all, flat, heads).reshape(tokens.shape)
+    heads_out = combine(*sums, heads)
+
     everyone = lax.all_gather(heads_out, "col", axis=0, tiled=True)
     terms = jnp.concatenate(
         [dot(everyone[:, t * hd : (t + 1) * hd], w_out).astype(BF16) for t in range(2)], axis=1

time: 288 us -> 261 us (0.906); the launches traced: 287 us -> 256 us
  Pallas kernels: 213 us -> 192 us
  waiting for transfers between devices: 15.1 us -> 7.95 us
    pallas_call x3 -> x1, Pallas kernels: 78.9 us -> 57.8 us  [back(): pl.pallas_call(functools.partial(back_kernel, heads), in_specs=[pl.BlockS...]
    all_to_all x1, waiting for transfers between devices: 8.49 us -> 0.01 us  [body(): lax.all_to_all(outgoing.reshape(holders, capacity * per, 2 * hf), axes, s...]
    unnamed x55 -> x49, local copies, waits for them, and re-layouts: 11.1 us -> 10.4 us
  transfers between devices with their start and end apart: 4 -> 4, of which waited for: 2 -> 1; matrix products, arithmetic and copies ran while one was open for 6% -> 6% of each run, Pallas kernels for 41% -> 45%
where the time goes in v4:
time: 261 us; the launch traced here: 256 us
  Pallas kernels  192 us (74%)
  local copies, waits for them, and re-layouts  27.3 us (10%)
  starting transfers between devices  19.4 us (7%)
  waiting for transfers between devices  7.95 us (3%)
  other arithmetic  5.4 us (2%)
  matrix products  4.36 us (2%)
    pallas_call x1, Pallas kernels, front(): pl.pallas_call(front_kernel, in_specs=[pl.BlockSpec(memory_space=pl.ANY)]...  62.8 us
    pallas_call x1, Pallas kernels, back(): pl.pallas_call(functools.partial(back_kernel, heads), in_specs=[pl.BlockS...  57.8 us
    pallas_call x1, Pallas kernels, tail_terms(): pl.pallas_call(functools.partial(tail_kernel, heads, tail), grid=(conts /...  26.2 us
    pallas_call x1, Pallas kernels, turn_states(): pl.pallas_call(state_kernel, grid=(heads,), in_specs=[pl.BlockSpec((width...  18.5 us
    pallas_call x1, Pallas kernels, prompt_terms(): pl.pallas_call(prompt_kernel, grid=(heads,), in_specs=[pl.BlockSpec(slot_...  17.9 us
    unnamed x49, local copies, waits for them, and re-layouts  10.4 us
    pallas_call x1, Pallas kernels, project(): pl.pallas_call(project_kernel, grid=(conts // block,), in_specs=[pl.Block...  8.61 us
    all_to_all x1, waiting for transfers between devices, body(): lax.all_to_all(replies.reshape(holders, capacity * per, -1), axes, split_...  7.94 us
  transfers between devices with their start and end apart: 4, of which 1 were waited for; matrix products, arithmetic and copies ran while one was open for 6% of the time, Pallas kernels for 45%

profile of v4, /device:TPU:9, one launch (start us, length us, event | category | flops | bytes accessed | tf_op | source)
XLA Modules:
  0.0 256.5 jit_solution(9350004110781375422)
XLA Ops:
  0.0 1.3 broadcast_in_dim.43
  1.3 6.6 %all-to-all-start = ((s32[16,1,32]{2,1,0:T(1,128)}), s32[16,1,32]{2,1,0:T(1,128)S(1)}, u32[]{:S(2)}, u32[]{:S(2)}) async-start(s32[16,1,32]{2,1,0:T(1,128)} %broadcast_in_dim.43), calls=%async_computation | async-start | bytes 16384 | tf_op jit(solution)/shard_map/all_to_all | solution.py:624
  8.6 3.8 %copy.77.x = bf16[1024,896]{1,0:T(8,128)(2,1)} copy(bf16[1024,896]{0,1:T(8,128)(2,1)} %bitcast.27) | data formatting | bytes 3670016 | tf_op jit(solution)/shard_map/reshape | solution.py:625
  12.4 1.3 reshape.296
  15.1 1.1 pad_maximum_fusion.1.w
  16.2 62.8 %shard_map.226 = (bf16[4,512,896]{2,1,0:T(8,128)(2,1)}, bf16[4,448,1152]{2,1,0:T(8,128)(2,1)}, bf16[1024,896]{1,0:T(8,128)(2,1)}) custom-call(bf16[1024,896]{1,0:T(8,128)(2,1)} %copy.77.x, bf16[448,1152]{1,0:T(8,128)(2,1)} %pad_maximum_fusion.1.w), custom_call_target="tpu_custom_call" | custom-call | tf_op jit(solution)/shard_map/pallas_call | solution.py:418
  79.0 2.0 copy-done.2
  81.0 8.6 %shard_map.227.q_ref = bf16[512,2304]{1,0:T(8,128)(2,1)S(1)} custom-call(bf16[4,512,896]{2,1,0:T(8,128)(2,1)S(1)} %copy-done.2, bf16[4,448,1152]{2,1,0:T(8,128)(2,1)} %get-tuple-element.12.w_ref), custom_call_target="tpu_custom_call" | custom-call | tf_op jit(solution)/shard_map/pallas_call | solution.py:584
  93.8 5.5 %all-to-all-start.1 = ((bf16[16,32,256]{2,1,0:T(8,128)(2,1)}), bf16[16,32,256]{2,1,0:T(8,128)(2,1)S(1)}, u32[]{:S(2)}, u32[]{:S(2)}) async-start(bf16[16,32,256]{2,1,0:T(8,128)(2,1)} %bitcast.9), calls=%async_computation.1 | async-start | bytes 524288 | tf_op jit(solution)/shard_map/all_to_all | solution.py:669
  99.3 18.5 %shard_map.229.states_ref = bf16[8,32,128,384]{3,2,1,0:T(8,128)(2,1)} custom-call(bf16[256,256]{1,0:T(8,128)(2,1)S(1)} %copy-done.15, bf16[1,273,28672]{2,1,0:T(8,128)(2,1)} %state_ref.1, bf16[8,32,273]{2,1,0:T(8,128)(2,1)S(1)} %bitcast.22), custom_call_target="tpu_custom_call" | custom-call | flops 20000000000 | bytes 45000000 | tf_op jit(solution)/shard_map/pallas_call | solution.py:64
  119.2 17.9 %shard_map.230.kept = bf16[512,2048]{1,0:T(8,128)(2,1)S(1)} custom-call(bf16[512,256]{1,0:T(8,128)(2,1)S(1)} %fusion.q_ref, bf16[8,128,768]{2,1,0:T(8,128)(2,1)S(1)} %copy-done.5, f32[8,384]{1,0:T(8,128)S(1)} %copy-done.6, bf16[8,32,128,384]{3,2,1,0:T(8,128)(2,1)} %shard_map.229.states_ref), custom_call_target="tpu_custom_call" | custom-call | tf_op jit(solution)/shard_map/pallas_call | solution.py:132
  137.1 2.7 %convolution_convert_fusion = bf16[512,2048]{1,0:T(8,128)(2,1)} fusion(bf16[512,2048]{1,0:T(8,128)(2,1)S(1)} %shard_map.230.kept, s32[512]{0:T(512)S(1)} %select_n.139), kind=kOutput, calls=%fused_computation | convolution fusion | flops 1075052544 | bytes 4196352 | tf_op jit(solution)/shard_map/dot_general | solution.py:22
  139.8 6.3 %all-to-all-start.2 = ((bf16[16,32,2048]{2,1,0:T(8,128)(2,1)}), bf16[16,32,2048]{2,1,0:T(8,128)(2,1)}, u32[]{:S(2)}, u32[]{:S(2)}) async-start(bf16[16,32,2048]{2,1,0:T(8,128)(2,1)} %bitcast.26), calls=%async_computation.2 | async-start | bytes 4194304 | tf_op jit(solution)/shard_map/all_to_all | solution.py:677
  147.3 1.2 copy-done.9
  148.5 1.0 copy-done.10
  152.2 26.2 %shard_map.228.acc = f32[512,2048]{1,0:T(8,128)} custom-call(bf16[512,2304]{1,0:T(8,128)(2,1)} %copy-done.3, bf16[512,1024]{1,0:T(8,128)(2,1)S(1)} %copy-done.7, bf16[512,7168]{1,0:T(8,128)(2,1)} %tv_ref.1, s32[512,1]{1,0:T(8,128)S(1)} %copy.78.len_ref, bf16[128,1024]{1,0:T(8,128)(2,1)S(1)} %copy-done.11, bf16[1024,64]{1,0:T(8,128)(2,1)S(1)} %copy-done.12, ...), custom_call_target="tpu_custom_call" | custom-call | flops 20000000000 | bytes 25000000 | tf_op jit(solution)/shard_map/pallas_call | solution.py:222
  178.3 1.5 copy.87
  180.6 2.3 copy.88
  182.8 1.4 pad_maximum_fusion.w
  184.2 7.9 %all-to-all-done.2 = bf16[16,32,2048]{2,1,0:T(8,128)(2,1)} async-done(((bf16[16,32,2048]{2,1,0:T(8,128)(2,1)}), bf16[16,32,2048]{2,1,0:T(8,128)(2,1)}, u32[]{:S(2)}, u32[]{:S(2)}) %all-to-all-start.2) | async-done | bytes 2097184 | tf_op jit(solution)/shard_map/all_to_all | solution.py:677
  192.2 1.5 copy-done.4
  193.7 57.8 %shard_map.231 = bf16[1024,896]{1,0:T(8,128)(2,1)S(1)} custom-call(f32[512,2048]{1,0:T(8,128)} %shard_map.228.acc, s32[512,1]{1,0:T(8,128)S(1)} %get-tuple-element.24.sent_at, s32[512,1]{1,0:T(8,128)S(1)} %get-tuple-element.23.kept_at, bf16[512,2048]{1,0:T(8,128)(2,1)} %bitcast.12.got, bf16[512,2048]{1,0:T(8,128)(2,1)} %copy-done, ...), custom_call_target="tpu_custom_call" | custom-call | tf_op jit(solution)/shard_map/pallas_call | solution.py:559
  251.4 1.2 copy-done.1
  252.7 3.8 %copy.90 = bf16[1024,896]{0,1:T(8,128)(2,1)} copy(bf16[1024,896]{1,0:T(8,128)(2,1)} %copy-done.1) | data formatting | bytes 3670016 | tf_op jit(solution)/shard_map/pallas_call | solution.py:559
  (76 shorter events, 12.0 us)
Async XLA Ops:
  0.0 12.4 %copy-start.17 = (bf16[8,50176]{1,0:T(8,128)(2,1)S(1)}, bf16[8,50176]{1,0:T(8,128)(2,1)}, u32[]{:S(2)}) copy-start(bf16[8,50176]{1,0:T(8,128)(2,1)} %param.27) | copy-start | bytes 2408452
  1.3 88.8 %all-to-all-start = ((s32[16,1,32]{2,1,0:T(1,128)}), s32[16,1,32]{2,1,0:T(1,128)S(1)}, u32[]{:S(2)}, u32[]{:S(2)}) async-start(s32[16,1,32]{2,1,0:T(1,128)} %broadcast_in_dim.43), calls=%async_computation | async-start | bytes 16384 | tf_op jit(solution)/shard_map/all_to_all | solution.py:624
  13.7 1.4 copy-start.19
  13.7 1.4 copy-start.20
  79.0 2.0 copy-start.2
  81.0 8.9 %copy-start.23 = (s32[32]{0:T(128)S(1)}, s32[32]{0:T(128)}, u32[]{:S(2)}) copy-start(s32[32]{0:T(128)} %param.31) | copy-start | bytes 388
  81.0 8.9 %copy-start.21 = (s32[512]{0:T(512)S(1)}, s32[512]{0:T(512)}, u32[]{:S(2)}) copy-start(s32[512]{0:T(512)} %param.32) | copy-start | bytes 6148
  81.0 9.0 %copy-start.18 = (bf16[32,273,8]{1,2,0:T(8,128)(2,1)S(1)}, bf16[32,273,8]{1,2,0:T(8,128)(2,1)}, u32[]{:S(2)}) copy-start(bf16[32,273,8]{1,2,0:T(8,128)(2,1)} %param.30) | copy-start | bytes 419332
  89.7 28.1 %copy-start.3 = (bf16[512,2304]{1,0:T(8,128)(2,1)}, bf16[512,2304]{1,0:T(8,128)(2,1)S(1)}, u32[]{:S(2)}) copy-start(bf16[512,2304]{1,0:T(8,128)(2,1)S(1)} %shard_map.227.q_ref) | copy-start | bytes 7077892
  89.7 9.6 %copy-start.15 = (bf16[256,256]{1,0:T(8,128)(2,1)S(1)}, bf16[256,256]{1,0:T(8,128)(2,1)}, u32[]{:S(2)}) copy-start(bf16[256,256]{1,0:T(8,128)(2,1)} %constant.99.clone.perm_ref) | copy-start | bytes 393220
  93.8 24.0 %all-to-all-start.1 = ((bf16[16,32,256]{2,1,0:T(8,128)(2,1)}), bf16[16,32,256]{2,1,0:T(8,128)(2,1)S(1)}, u32[]{:S(2)}, u32[]{:S(2)}) async-start(bf16[16,32,256]{2,1,0:T(8,128)(2,1)} %bitcast.9), calls=%async_computation.1 | async-start | bytes 524288 | tf_op jit(solution)/shard_map/all_to_all | solution.py:669
  99.3 19.2 %copy-start.6 = (f32[8,384]{1,0:T(8,128)S(1)}, f32[8,384]{1,0:T(8,128)}, u32[]{:S(2)}) copy-start(f32[8,384]{1,0:T(8,128)} %constant.109.clone.shift_ref) | copy-start | bytes 36868
  117.8 1.4 copy-start.5
  137.1 2.7 %copy-start = (bf16[512,2048]{1,0:T(8,128)(2,1)}, bf16[512,2048]{1,0:T(8,128)(2,1)S(1)}, u32[]{:S(2)}) copy-start(bf16[512,2048]{1,0:T(8,128)(2,1)S(1)} %shard_map.230.kept) | copy-start | bytes 6291460
  139.8 7.4 %copy-start.22 = (s32[512]{0:T(512)S(1)}, s32[512]{0:T(512)}, u32[]{:S(2)}) copy-start(s32[512]{0:T(512)} %param.35) | copy-start | bytes 6148
  139.8 7.5 %copy-start.7 = (bf16[512,1024]{1,0:T(8,128)(2,1)S(1)}, bf16[512,1024]{1,0:T(8,128)(2,1)}, u32[]{:S(2)}) copy-start(bf16[512,1024]{1,0:T(8,128)(2,1)} %tk_ref.1) | copy-start | bytes 3145732
  139.8 7.5 %copy-start.8 = (bf16[896,1024]{1,0:T(8,128)(2,1)S(1)}, bf16[896,1024]{1,0:T(8,128)(2,1)}, u32[]{:S(2)}) copy-start(bf16[896,1024]{1,0:T(8,128)(2,1)} %constant.107.clone.pad) | copy-start | bytes 5505028
  139.8 7.5 %copy-start.11 = (bf16[128,1024]{1,0:T(8,128)(2,1)S(1)}, bf16[128,1024]{1,0:T(8,128)(2,1)}, u32[]{:S(2)}) copy-start(bf16[128,1024]{1,0:T(8,128)(2,1)} %constant.100.clone.eq) | copy-start | bytes 786436
  139.8 7.5 %copy-start.14 = (bf16[64,1024]{1,0:T(8,128)(2,1)S(1)}, bf16[64,1024]{1,0:T(8,128)(2,1)}, u32[]{:S(2)}) copy-start(bf16[64,1024]{1,0:T(8,128)(2,1)} %constant.104.clone.dw) | copy-start | bytes 393220
  139.8 52.4 %all-to-all-start.2 = ((bf16[16,32,2048]{2,1,0:T(8,128)(2,1)}), bf16[16,32,2048]{2,1,0:T(8,128)(2,1)}, u32[]{:S(2)}, u32[]{:S(2)}) async-start(bf16[16,32,2048]{2,1,0:T(8,128)(2,1)} %bitcast.26), calls=%async_computation.2 | async-start | bytes 4194304 | tf_op jit(solution)/shard_map/all_to_all | solution.py:677
  146.1 34.5 %collective-permute-start = (bf16[896,448]{0,1:T(8,128)(2,1)}, bf16[896,448]{0,1:T(8,128)(2,1)}, u32[]{:S(2)}, u32[]{:S(2)}) collective-permute-start(bf16[896,448]{0,1:T(8,128)(2,1)} %param.28), channel_id=1, source_target_pairs={{0,4},{4,0},{1,5},{5,1},{2,6},{6,2},{3,7},{7,3},{8,12},{12,8},{9,1... | collective-permute-start | bytes 2408456 | tf_op jit(solution)/shard_map/ppermute | solution.py:632
  147.3 1.2 copy-start.9
  192.2 1.5 copy-start.4
  251.4 1.2 copy-start.1
  (4 other events, 3.7 us)
